TPU v7x, 768 devices: a whole 4x8x12 slice. The times are simulated.
768 devices in a mesh: rep: 48 (over x, z_lo, core), fsdp: 16 (over y, z_hi).
Axes of the slice: x: 4, y: 8, z: 12 (z_hi: 2, z_lo: 6; z = z_hi * 6 + z_lo), core: 2. Of those that a mesh axis runs over, the one named last changes fastest.
Arguments:
- attn_heads: bfloat16 [196608, 2560], P(('rep', 'fsdp')), may hold values from -6 to 6
- proj_weight: bfloat16 [48, 2560, 2560], P('rep', 'fsdp'), may hold values from -0.125 to 0.125
- base_frag: bfloat16 [768, 5120], P('fsdp'), may hold values from -6 to 6
- local_frag: bfloat16 [48, 768, 5120], P('rep', 'fsdp'), may hold values from -6 to 6
- block_exps: int32 [48, 768, 40], P('rep', 'fsdp'), may hold values from -2 to 2
- momentum: float32 [768, 5120], P('fsdp'), may hold values from -6 to 6
Outputs:
- mixed: bfloat16 [196608, 2560], P(('rep', 'fsdp'))
- new_base: bfloat16 [768, 5120], P('fsdp')
- new_momentum: float32 [768, 5120], P('fsdp')
All inputs are finite; a program needn't handle non-finite values.
Results may differ from a plain program's by a relative error of at most 0.0028.
Values may be sent and summed in bfloat16 or wider, within the bound.
No kernel may reach another device: no remote copies, remote signals or barrier semaphores. Data moves between devices by JAX's collectives and lax.ppermute only.
A program may use at most 64 MiB of HBM per device.

v0:
```python
import jax
import jax.numpy as jnp
from jax import lax
from jax.sharding import PartitionSpec as P


def per_device(attn_heads, proj_weight, base_frag, local_frag, block_exps, momentum):
    mixed = jnp.dot(
        attn_heads,
        lax.all_gather(proj_weight[0], "fsdp", axis=0, tiled=True),
        preferred_element_type=jnp.float32,
    ).astype(jnp.bfloat16)
    base_wide = base_frag.astype(jnp.float32)
    scale = jnp.repeat(jnp.exp2(block_exps[0].astype(jnp.float32)), 128, axis=1)
    inverse = jnp.repeat(jnp.exp2(-block_exps[0].astype(jnp.float32)), 128, axis=1)
    level = jnp.clip((base_wide - local_frag[0].astype(jnp.float32)) * inverse, -1.0, 1.0)
    level = lax.optimization_barrier(level.astype(jnp.bfloat16)).astype(jnp.float32)
    term = (level * scale).reshape(-1, 128)
    base_blocks = base_wide.reshape(-1, 128)
    moment_blocks = momentum.reshape(-1, 128)
    replicas = lax.axis_size("rep")
    share = term.shape[0] // replicas
    offset = lax.axis_index("rep") * share
    outer_grad = lax.psum_scatter(term, "rep", scatter_dimension=0, tiled=True) / replicas
    own_moment = lax.dynamic_slice_in_dim(moment_blocks, offset, share, 0)
    own_base = lax.dynamic_slice_in_dim(base_blocks, offset, share, 0)
    moment_part = 0.9 * own_moment + outer_grad
    base_part = (own_base - 0.7 * (outer_grad + 0.9 * moment_part)).astype(jnp.bfloat16)
    new_base = lax.all_gather(base_part, "rep", axis=0, tiled=True).reshape(base_frag.shape)
    new_momentum = lax.all_gather(moment_part, "rep", axis=0, tiled=True).reshape(momentum.shape)
    return (mixed, new_base, new_momentum)


def solution(mesh):
    return jax.shard_map(
        per_device,
        mesh=mesh,
        in_specs=(
            P(("rep", "fsdp"), None),
            P("rep", "fsdp", None),
            P("fsdp", None),
            P("rep", "fsdp", None),
            P("rep", "fsdp", None),
            P("fsdp", None),
        ),
        out_specs=(P(("rep", "fsdp"), None), P("fsdp", None), P("fsdp", None)),
        check_vma=False,
    )
```

profile of v0, /device:TPU:1, one launch (start us, length us, event | category | flops | bytes accessed | tf_op | source)
XLA Modules:
  0.0 715.4 jit_solution(67522663475953430)
XLA Ops:
  8.0 0.0 copy-start
  8.0 0.0 copy-start.2
  8.0 0.0 copy-start.1
  8.0 0.0 reduce-scatter.5.cloned.1.call-start
  8.1 0.9 exponential_bitcast_fusion.1
  9.0 0.1 copy.12
  9.0 0.1 copy.11
  9.1 0.3 broadcast_in_dim.6
  9.4 0.0 copy-done.2
  9.5 0.0 copy-done.1
  9.5 0.3 fusion.6
  9.7 0.3 broadcast_in_dim.7
  10.0 0.2 bitcast_multiply_fusion
  10.3 1.1 reshape.40
  11.3 0.0 reduce-scatter.5.cloned.1.call-update
  11.4 0.0 all-gather.3.cloned.1.call-start
  11.4 0.5 all-gather.3.cloned.1.call-update
  12.0 0.2 reshape.37
  12.2 1.4 reshape.41
  13.5 518.1 %reduce-scatter.5.cloned.1.call-done = f32[40,128]{1,0:T(8,128)} async-done(((f32[1920,128]{1,0:T(8,128)}), f32[40,128]{1,0:T(8,128)}) %reduce-scatter.5.cloned.1.call-update) | async-done | bytes 20496
  531.6 0.7 multiply_add_fusion
  532.4 84.6 %all_gather.10 = bf16[1920,128]{1,0:T(8,128)(2,1)S(1)} all-gather(bf16[40,128]{1,0:T(8,128)(2,1)S(1)} %get-tuple-element.4), channel_id=1, replica_groups=mesh['rep'=48,'fsdp'=16] {'rep'}, dimensions={0}, use_global_device_ids=true | all-gather | bytes 501760 | tf_op jit(solution)/shard_map/all_gather | solution.py:29
  617.0 1.0 reshape.42
  618.0 79.6 %all_gather.11 = f32[1920,128]{1,0:T(8,128)S(1)} all-gather(f32[40,128]{1,0:T(8,128)S(1)} %get-tuple-element.3), channel_id=1, replica_groups=mesh['rep'=48,'fsdp'=16] {'rep'}, dimensions={0}, use_global_device_ids=true | all-gather | bytes 1003520 | tf_op jit(solution)/shard_map/all_gather | solution.py:30
  697.6 1.1 reshape.43
  698.7 0.0 all-gather.3.cloned.1.call-done
  698.7 0.0 copy-done
  698.7 9.3 %fusion.2 = bf16[256,2560]{1,0:T(8,128)(2,1)} fusion(bf16[256,2560]{1,0:T(8,128)(2,1)S(1)} %copy-done, bf16[1,2560,2560]{2,1,0:T(8,128)(2,1)} %all-gather.3.cloned.1.call-done), kind=kOutput, calls=%fused_computation.2 | convolution fusion | flops 3356098560 | bytes 15728640 | tf_op jit(solution)/shard_map/dot_general | solution.py:8
Async XLA Ops:
  8.0 690.7 %copy-start = (bf16[256,2560]{1,0:T(8,128)(2,1)S(1)}, bf16[256,2560]{1,0:T(8,128)(2,1)}, u32[]{:S(2)}) copy-start(bf16[256,2560]{1,0:T(8,128)(2,1)} %param.6) | copy-start | bytes 3932164
  8.0 1.4 copy-start.2
  8.0 1.4 copy-start.1
  8.0 523.6 %reduce-scatter.5.cloned.1.call-start = ((), (), s32[]{:S(2)}) async-start(), calls=%async_computation.2 | async-start | bytes 1003520
  11.4 687.3 %all-gather.3.cloned.1.call-start = ((), (), s32[]{:S(2)}) async-start(), calls=%async_computation.1 | async-start | bytes 13926400 | tf_op jit(solution)/shard_map/all_gather | solution.py:10
Sparse Core Ops, SparseCore 0:
  12.5 519.0 reduce-scatter.4
Sparse Core Ops, SparseCore 1:
  15.6 310.3 all-gather.2
where the time goes:
time: 716 us; the launch traced here: 715 us
  waiting for transfers between devices  519 us (72%)
  blocking collectives  164 us (23%)
  between operations  15.6 us (2%)
  matrix products  9.32 us (1%)
    unnamed x3, waiting for transfers between devices  519 us
    all_gather x1, blocking collectives, per_device(): lax.all_gather(base_part, 'rep', axis=0, tiled=True)  84.6 us
    all_gather x1, blocking collectives, per_device(): lax.all_gather(moment_part, 'rep', axis=0, tiled=True)  79.6 us
  transfers between devices with their start and end apart: 2, of which 1 were waited for; matrix products, arithmetic and copies ran while one was open for 1% of the time, Pallas kernels for 0%

commit v1 on v0

v1 whole, which is shorter than its diff:
```python
import jax
import jax.numpy as jnp
from jax import lax
from jax.experimental import pallas as pl
from jax.experimental.pallas import tpu as pltpu
from jax.sharding import PartitionSpec as P

HALF = 80
Y, ZH, ZL, X, C = 8, 2, 6, 4, 2


def moved(to):
    def place(x, y, z, c):
        return (((x * ZL + z % ZL) * C + c) * Y + y) * ZH + z // ZL

    return [
        (place(x, y, z, c), place(*to(x, y, z, c)))
        for x in range(X)
        for y in range(Y)
        for z in range(ZL * ZH)
        for c in range(C)
    ]


UP = moved(lambda x, y, z, c: (x, (y + 1) % Y, z, c))
DOWN = moved(lambda x, y, z, c: (x, (y - 1) % Y, z, c))
AHEAD = moved(lambda x, y, z, c: (x, y, (z + 2) % (ZL * ZH), c))
BACK = moved(lambda x, y, z, c: (x, y, (z - 2) % (ZL * ZH), c))
CORE = moved(lambda x, y, z, c: (x, y, z, 1 - c))
X_FAR = moved(lambda x, y, z, c: (x ^ 2, y, z, c))
X_NEAR = moved(lambda x, y, z, c: (x ^ 1, y, z, c))
Z_PAIR = moved(lambda x, y, z, c: (x, y, z ^ 1, c))
Z_TWO = moved(lambda x, y, z, c: (x, y, (z // ZL) * ZL + (z % ZL + 2) % ZL, c))
Z_FOUR = moved(lambda x, y, z, c: (x, y, (z // ZL) * ZL + (z % ZL + 4) % ZL, c))


def send_to(array, pairs):
    return lax.ppermute(array, ("rep", "fsdp"), pairs)


def product(slots, tokens, picks, weights, total, out_dtype):
    rows, width = tokens.shape[1], weights[0].shape[1]
    tile, count = 512, len(weights)

    def kernel(slots_ref, *refs):
        del slots_ref
        out = refs[-1]
        acc = jnp.zeros((rows, tile), jnp.float32) if total is None else refs[-2][...]
        for block, weight in zip(refs[:count], refs[count : 2 * count]):
            acc += jnp.dot(block[0], weight[...], preferred_element_type=jnp.float32)
        out[...] = acc.astype(out_dtype)

    def block_of(slot):
        return pl.BlockSpec((1,) + tokens.shape[1:], lambda j, at: (at[slot], 0, 0))

    in_specs = [block_of(slot) for slot in picks]
    in_specs += [pl.BlockSpec((w.shape[0], tile), lambda j, at: (0, j)) for w in weights]
    operands = [slots] + [tokens] * count + list(weights)
    if total is not None:
        in_specs.append(pl.BlockSpec((rows, tile), lambda j, at: (0, j)))
        operands.append(total)
    depth = sum(w.shape[0] for w in weights)
    return pl.pallas_call(
        kernel,
        grid_spec=pltpu.PrefetchScalarGridSpec(
            num_scalar_prefetch=1,
            grid=(width // tile,),
            in_specs=in_specs,
            out_specs=pl.BlockSpec((rows, tile), lambda j, at: (0, j)),
        ),
        out_shape=jax.ShapeDtypeStruct((rows, width), out_dtype),
        compiler_params=pltpu.CompilerParams(vmem_limit_bytes=24 << 20),
        cost_estimate=pl.CostEstimate(
            flops=2 * rows * width * depth,
            bytes_accessed=2 * width * depth + 6 * rows * width,
            transcendentals=0,
        ),
    )(*operands)


def fragment_term(base_wide, local_frag, block_exps):
    exps = block_exps.astype(jnp.float32)
    scale = jnp.repeat(jnp.exp2(exps), 128, axis=1)
    inverse = jnp.repeat(jnp.exp2(-exps), 128, axis=1)
    level = jnp.clip((base_wide - local_frag.astype(jnp.float32)) * inverse, -1.0, 1.0)
    return level.astype(jnp.bfloat16) * scale.astype(jnp.bfloat16)


def keep_and_send(array, index, axis):
    half = array.shape[axis] // 2
    first = lax.slice_in_dim(array, 0, half, axis=axis)
    second = lax.slice_in_dim(array, half, 2 * half, axis=axis)
    return jnp.where(index == 0, first, second), jnp.where(index == 0, second, first)


def join(mine, other, index, axis):
    return jnp.concatenate(
        [jnp.where(index == 0, mine, other), jnp.where(index == 0, other, mine)], axis=axis
    )


def together(*arrays):
    return lax.optimization_barrier(arrays)


def per_device(attn_heads, proj_weight, base_frag, local_frag, block_exps, momentum):
    own = proj_weight[0]
    index = lax.axis_index("fsdp")
    y, h = index // ZH, index % ZH
    index = lax.axis_index("rep")
    core, z, x = index % C, (index // C) % ZL, index // (C * ZL)
    far, near, third = x // 2, x % 2, z // 2
    base_wide = base_frag.astype(jnp.float32)

    up1, down1 = send_to(own, UP), send_to(own, DOWN)
    ahead, back = send_to(own[:HALF], AHEAD), send_to(own[HALF:], BACK)
    keep, give = keep_and_send(fragment_term(base_wide, local_frag[0], block_exps[0]), core, 0)
    part = keep.astype(jnp.float32) + send_to(give, CORE).astype(jnp.float32)
    up1, down1, ahead, back, part = together(up1, down1, ahead, back, part)

    up2, down2 = send_to(up1, UP), send_to(down1, DOWN)
    ahead, back = send_to(ahead, AHEAD), send_to(back, BACK)
    keep, give = keep_and_send(part, far, 1)
    part = keep + send_to(give, X_FAR)
    up2, down2, ahead, back, part = together(up2, down2, ahead, back, part)

    up3, down3 = send_to(up2, UP), send_to(down2, DOWN)
    ahead, back = send_to(ahead, AHEAD), send_to(back, BACK)
    keep, give = keep_and_send(part, near, 1)
    part = keep + send_to(give, X_NEAR)
    up3, down3, ahead, back, part, heads = together(up3, down3, ahead, back, part, attn_heads)
    other = jnp.concatenate([ahead, back], axis=0)

    up4, over_down1 = send_to(up3, UP), send_to(other, DOWN)
    part = part + send_to(part, Z_PAIR)
    rows = attn_heads.shape[0]
    tokens = heads.reshape(rows, Y * ZH, 2 * HALF).transpose(1, 0, 2)
    turn = ((y + jnp.arange(Y)) % Y) * ZH
    slots = jnp.concatenate([turn + h, turn + (1 - h)]).astype(jnp.int32)
    up4, over_down1, part, tokens, other = together(up4, over_down1, part, tokens, other)

    over_up1, over_down2 = send_to(other, UP), send_to(over_down1, DOWN)
    two, four = send_to(part, Z_TWO), send_to(part, Z_FOUR)
    zero = jnp.where(third == 0, part, jnp.where(third == 1, two, four))
    one = jnp.where(third == 1, part, jnp.where(third == 2, two, four))
    last = jnp.where(third == 2, part, jnp.where(third == 0, two, four))
    part = (zero + one) + last
    total = product(
        slots,
        tokens,
        (0, 7, 1, 6, 2, 5, 3, 4),
        [own, up1, down1, up2, down2, up3, down3, up4],
        None,
        jnp.float32,
    )
    over_up1, over_down2, part, total = together(over_up1, over_down2, part, total)

    over_up2, over_down3 = send_to(over_up1, UP), send_to(over_down2, DOWN)
    part = join(part, send_to(part, X_NEAR), near, 1)
    part = join(part, send_to(part, X_FAR), far, 1)
    over_up2, over_down3, part = together(over_up2, over_down3, part)

    over_up3, over_down4 = send_to(over_up2, UP), send_to(over_down3, DOWN)
    outer_grad = join(part, send_to(part, CORE), core, 0) / (X * ZL * C)
    new_momentum = 0.9 * momentum + outer_grad
    new_base = (base_wide - 0.7 * (outer_grad + 0.9 * new_momentum)).astype(jnp.bfloat16)
    total = product(
        slots,
        tokens,
        (8, 15, 9, 14, 10, 11),
        [other, over_up1, over_down1, over_up2, over_down2, over_down3],
        total,
        jnp.float32,
    )
    over_up3, over_down4, total, new_momentum, new_base = together(
        over_up3, over_down4, total, new_momentum, new_base
    )
    mixed = product(slots, tokens, (13, 12), [over_up3, over_down4], total, jnp.bfloat16)
    return mixed, new_base, new_momentum


def solution(mesh):
    return jax.shard_map(
        per_device,
        mesh=mesh,
        in_specs=(
            P(("rep", "fsdp"), None),
            P("rep", "fsdp", None),
            P("fsdp", None),
            P("rep", "fsdp", None),
            P("rep", "fsdp", None),
            P("fsdp", None),
        ),
        out_specs=(P(("rep", "fsdp"), None), P("fsdp", None), P("fsdp", None)),
        check_vma=False,
    )
```

time: 716 us -> 236 us (0.33)
  waiting for transfers between devices: 519 us -> 83.1 us
  blocking collectives: 164 us -> 0 us
  starting transfers between devices: 0.08 us -> 115 us
  Pallas kernels: 0 us -> 15.5 us
  between operations: 15.6 us -> 1.28 us
  matrix products: 9.32 us -> 0 us
  local copies, waits for them, and re-layouts: 5.53 us -> 14 us
    unnamed x3 -> x0, waiting for transfers between devices: 519 us -> none
    all_gather x2 -> x0, blocking collectives: 164 us -> none  [the longest x1 84.6 us: per_device(): lax.all_gather(base_part, 'rep', axis=0, tiled=True)]
    ppermute x0 -> x29, starting transfers between devices: none -> 115 us  [send_to(): return lax.ppermute(array, ('rep', 'fsdp'), pairs)]
    ppermute x0 -> x29, waiting for transfers between devices: none -> 83.1 us  [send_to(): return lax.ppermute(array, ('rep', 'fsdp'), pairs)]
    pallas_call x0 -> x3, Pallas kernels: none -> 15.5 us  [product(): pl.pallas_call(kernel, grid_spec=pltpu.PrefetchScalarGridSpec(num_scalar_...]
    dot_general x1 -> x0, matrix products: 9.32 us -> none  [per_device(): jnp.dot(attn_heads, lax.all_gather(proj_weight[0], 'fsdp', axis=0, tiled=...]
  transfers between devices with their start and end apart: 2 -> 29, of which waited for: 1 -> 13; matrix products, arithmetic and copies ran while one was open for 1% -> 5% of each run, Pallas kernels for 0% -> 5%
where the time goes in v1:
time: 236 us; the launch traced here: 234 us
  starting transfers between devices  115 us (49%)
  waiting for transfers between devices  83.1 us (35%)
  Pallas kernels  15.5 us (7%)
  local copies, waits for them, and re-layouts  14 us (6%)
  other arithmetic  5.09 us (2%)
    ppermute x29, starting transfers between devices, send_to(): return lax.ppermute(array, ('rep', 'fsdp'), pairs)  115 us
    ppermute x29, waiting for transfers between devices, send_to(): return lax.ppermute(array, ('rep', 'fsdp'), pairs)  83.1 us
    pallas_call x3, Pallas kernels, product(): pl.pallas_call(kernel, grid_spec=pltpu.PrefetchScalarGridSpec(num_scalar_...  15.5 us
    unnamed x19, local copies, waits for them, and re-layouts  6.4 us
  transfers between devices with their start and end apart: 29, of which 13 were waited for; matrix products, arithmetic and copies ran while one was open for 5% of the time, Pallas kernels for 5%

profile of v1, /device:TPU:1, one launch (start us, length us, event | category | flops | bytes accessed | tf_op | source)
XLA Modules:
  0.0 234.3 jit_solution(10597102113035018583)
XLA Ops:
  0.6 5.9 %collective-permute-start.1 = (bf16[160,2560]{1,0:T(8,128)(2,1)}, bf16[160,2560]{1,0:T(8,128)(2,1)S(1)}, u32[]{:S(2)}, u32[]{:S(2)}) collective-permute-start(bf16[160,2560]{1,0:T(8,128)(2,1)} %bitcast.38), channel_id=1, source_target_pairs={{0,14},{16,30},{32,46},{48,62},{64,78},{80,94},{96,110},{112,126},... | collective-permute-start | bytes 2457608 | tf_op jit(solution)/shard_map/ppermute | solution.py:38
  11.6 10.4 %collective-permute-start.4 = (bf16[24,5120]{1,0:T(8,128)(2,1)S(1)}, bf16[24,5120]{1,0:T(8,128)(2,1)}, u32[]{:S(2)}, u32[]{:S(2)}) collective-permute-start(bf16[24,5120]{1,0:T(8,128)(2,1)S(1)} %broadcast_select_fusion.2), channel_id=1, source_target_pairs={{0,16},{16,0},{32,48},{48,32},{64,80},{80,64},{96,112},{112,96},{1... | collective-permute-start | bytes 737288 | tf_op jit(solution)/shard_map/ppermute | solution.py:38
  23.0 6.7 %collective-permute-start.3 = (bf16[80,2560]{1,0:T(8,128)(2,1)}, bf16[80,2560]{1,0:T(8,128)(2,1)}, u32[]{:S(2)}, u32[]{:S(2)}) collective-permute-start(bf16[80,2560]{1,0:T(8,128)(2,1)} %get-tuple-element.73), channel_id=1, source_target_pairs={{0,129},{16,145},{32,161},{48,177},{64,0},{80,16},{96,32},{112,48}... | collective-permute-start | bytes 1228808 | tf_op jit(solution)/shard_map/ppermute | solution.py:38
  32.7 14.9 %collective-permute-done.3 = bf16[80,2560]{1,0:T(8,128)(2,1)} collective-permute-done((bf16[80,2560]{1,0:T(8,128)(2,1)}, bf16[80,2560]{1,0:T(8,128)(2,1)}, u32[]{:S(2)}, u32[]{:S(2)}) %collective-permute-start.3) | collective-permute-done | bytes 409632 | tf_op jit(solution)/shard_map/ppermute | solution.py:38
  47.6 5.9 %collective-permute-done.2 = bf16[80,2560]{1,0:T(8,128)(2,1)} collective-permute-done((bf16[80,2560]{1,0:T(8,128)(2,1)}, bf16[80,2560]{1,0:T(8,128)(2,1)}, u32[]{:S(2)}, u32[]{:S(2)}) %collective-permute-start.2) | collective-permute-done | bytes 409632 | tf_op jit(solution)/shard_map/ppermute | solution.py:38
  53.6 4.7 %collective-permute-start.9 = (f32[24,2560]{1,0:T(8,128)S(1)}, f32[24,2560]{1,0:T(8,128)S(1)}, u32[]{:S(2)}, u32[]{:S(2)}) collective-permute-start(f32[24,2560]{1,0:T(8,128)S(1)} %slice_select_fusion), channel_id=1, source_target_pairs={{0,384},{16,400},{32,416},{48,432},{64,448},{80,464},{96,480},{112... | collective-permute-start | bytes 737288 | tf_op jit(solution)/shard_map/ppermute | solution.py:38
  60.2 4.9 %collective-permute-start.6 = (bf16[160,2560]{1,0:T(8,128)(2,1)S(1)}, bf16[160,2560]{1,0:T(8,128)(2,1)}, u32[]{:S(2)}, u32[]{:S(2)}) collective-permute-start(bf16[160,2560]{1,0:T(8,128)(2,1)S(1)} %collective-permute-done.1.refs_10_), channel_id=1, source_target_pairs={{0,14},{16,30},{32,46},{48,62},{64,78},{80,94},{96,110},{112,126},... | collective-permute-start | bytes 2457608 | tf_op jit(solution)/shard_map/ppermute | solution.py:38
  67.0 5.5 %collective-permute-start.8 = (bf16[80,2560]{1,0:T(8,128)(2,1)}, bf16[80,2560]{1,0:T(8,128)(2,1)S(1)}, u32[]{:S(2)}, u32[]{:S(2)}) collective-permute-start(bf16[80,2560]{1,0:T(8,128)(2,1)} %collective-permute-done.3), channel_id=1, source_target_pairs={{0,129},{16,145},{32,161},{48,177},{64,0},{80,16},{96,32},{112,48}... | collective-permute-start | bytes 1228808 | tf_op jit(solution)/shard_map/ppermute | solution.py:38
  72.5 15.3 %collective-permute-done.7 = bf16[80,2560]{1,0:T(8,128)(2,1)S(1)} collective-permute-done((bf16[80,2560]{1,0:T(8,128)(2,1)}, bf16[80,2560]{1,0:T(8,128)(2,1)S(1)}, u32[]{:S(2)}, u32[]{:S(2)}) %collective-permute-start.7) | collective-permute-done | bytes 409632 | tf_op jit(solution)/shard_map/ppermute | solution.py:38
  87.8 2.3 collective-permute-done.8
  92.0 4.6 %collective-permute-start.11 = (bf16[160,2560]{1,0:T(8,128)(2,1)}, bf16[160,2560]{1,0:T(8,128)(2,1)S(1)}, u32[]{:S(2)}, u32[]{:S(2)}) collective-permute-start(bf16[160,2560]{1,0:T(8,128)(2,1)} %collective-permute-done.6.refs_12_), channel_id=1, source_target_pairs={{0,14},{16,30},{32,46},{48,62},{64,78},{80,94},{96,110},{112,126},... | collective-permute-start | bytes 2457608 | tf_op jit(solution)/shard_map/ppermute | solution.py:38
  100.8 6.3 %collective-permute-start.13 = (bf16[80,2560]{1,0:T(8,128)(2,1)S(1)}, bf16[80,2560]{1,0:T(8,128)(2,1)S(1)}, u32[]{:S(2)}, u32[]{:S(2)}) collective-permute-start(bf16[80,2560]{1,0:T(8,128)(2,1)S(1)} %collective-permute-done.8), channel_id=1, source_target_pairs={{0,129},{16,145},{32,161},{48,177},{64,0},{80,16},{96,32},{112,48}... | collective-permute-start | bytes 1228808 | tf_op jit(solution)/shard_map/ppermute | solution.py:38
  107.1 6.2 %collective-permute-done.12 = bf16[80,2560]{1,0:T(8,128)(2,1)S(1)} collective-permute-done((bf16[80,2560]{1,0:T(8,128)(2,1)S(1)}, bf16[80,2560]{1,0:T(8,128)(2,1)S(1)}, u32[]{:S(2)}, u32[]{:S(2)}) %collective-permute-start.12) | collective-permute-done | bytes 409632 | tf_op jit(solution)/shard_map/ppermute | solution.py:38
  113.2 4.2 %collective-permute-done.13 = bf16[80,2560]{1,0:T(8,128)(2,1)S(1)} collective-permute-done((bf16[80,2560]{1,0:T(8,128)(2,1)S(1)}, bf16[80,2560]{1,0:T(8,128)(2,1)S(1)}, u32[]{:S(2)}, u32[]{:S(2)}) %collective-permute-start.13) | collective-permute-done | bytes 409632 | tf_op jit(solution)/shard_map/ppermute | solution.py:38
  122.1 3.1 %collective-permute-start.15 = (bf16[160,2560]{1,0:T(8,128)(2,1)}, bf16[160,2560]{1,0:T(8,128)(2,1)}, u32[]{:S(2)}, u32[]{:S(2)}) collective-permute-start(bf16[160,2560]{1,0:T(8,128)(2,1)} %collective-permute-done.10.refs_13_), channel_id=1, source_target_pairs={{0,2},{16,18},{32,34},{48,50},{64,66},{80,82},{96,98},{112,114},{1... | collective-permute-start | bytes 2457608 | tf_op jit(solution)/shard_map/ppermute | solution.py:38
  127.3 2.4 %copy.13 = bf16[256,2560]{0,1:T(8,128)(2,1)} copy(bf16[256,2560]{1,0:T(8,128)(2,1)} %param.6) | data formatting | bytes 2621440 | tf_op jit(solution)/shard_map/optimization_barrier | solution.py:103
  129.7 2.7 %copy.14 = bf16[256,16,160]{2,0,1:T(8,128)(2,1)S(1)} copy(bf16[256,16,160]{0,2,1:T(8,128)(2,1)} %bitcast.41) | data formatting | bytes 2621440 | tf_op jit(solution)/shard_map/reshape | solution.py:137
  132.4 5.8 %collective-permute-done.16.refs_8_ = bf16[160,2560]{1,0:T(8,128)(2,1)} collective-permute-done((bf16[160,2560]{1,0:T(8,128)(2,1)}, bf16[160,2560]{1,0:T(8,128)(2,1)}, u32[]{:S(2)}, u32[]{:S(2)}) %collective-permute-start.16) | collective-permute-done | bytes 819232 | tf_op jit(solution)/shard_map/ppermute | solution.py:38
  138.2 3.1 %collective-permute-done.15.refs_15_ = bf16[160,2560]{1,0:T(8,128)(2,1)} collective-permute-done((bf16[160,2560]{1,0:T(8,128)(2,1)}, bf16[160,2560]{1,0:T(8,128)(2,1)}, u32[]{:S(2)}, u32[]{:S(2)}) %collective-permute-start.15) | collective-permute-done | bytes 819232 | tf_op jit(solution)/shard_map/ppermute | solution.py:38
  143.3 4.5 %collective-permute-start.19 = (bf16[160,2560]{1,0:T(8,128)(2,1)}, bf16[160,2560]{1,0:T(8,128)(2,1)S(1)}, u32[]{:S(2)}, u32[]{:S(2)}) collective-permute-start(bf16[160,2560]{1,0:T(8,128)(2,1)} %collective-permute-done.16.refs_8_), channel_id=1, source_target_pairs={{0,14},{16,30},{32,46},{48,62},{64,78},{80,94},{96,110},{112,126},... | collective-permute-start | bytes 2457608 | tf_op jit(solution)/shard_map/ppermute | solution.py:38
  147.9 9.6 %collective-permute-start.21 = (f32[24,1280]{1,0:T(8,128)S(1)}, f32[24,1280]{1,0:T(8,128)S(1)}, u32[]{:S(2)}, u32[]{:S(2)}) collective-permute-start(f32[24,1280]{1,0:T(8,128)S(1)} %add.79), channel_id=1, source_target_pairs={{0,128},{16,144},{32,160},{48,176},{64,0},{80,16},{96,32},{112,48}... | collective-permute-start | bytes 368648 | tf_op jit(solution)/shard_map/ppermute | solution.py:38
  162.9 6.4 %shard_map.85.refs_12_ = f32[256,2560]{1,0:T(8,128)S(1)} custom-call(s32[16]{0:T(128)S(1)} %pad_add_fusion.slots_ref, bf16[16,256,160]{2,1,0:T(8,128)(2,1)S(1)} %bitcast.22, bf16[16,256,160]{2,1,0:T(8,128)(2,1)S(1)} %bitcast.23, bf16[16,256,160]{2,1,0:T(8,128)(2,1)S(1)} %bitcast.24, bf16[16,256,160]{2,1,0:T(8,128)(2,1)S(1)} %bitcast.25, ...), custom_call_target="tpu_custom_call" | custom-call | flops 1677721600 | bytes 10485760 | tf_op jit(solution)/shard_map/pallas_call | solution.py:63
  169.4 3.1 %collective-permute-start.24 = (f32[24,1280]{1,0:T(8,128)S(1)}, f32[24,1280]{1,0:T(8,128)S(1)}, u32[]{:S(2)}, u32[]{:S(2)}) collective-permute-start(f32[24,1280]{1,0:T(8,128)S(1)} %select_add_fusion.1), channel_id=1, source_target_pairs={{0,192},{16,208},{32,224},{48,240},{64,256},{80,272},{96,288},{112... | collective-permute-start | bytes 368648 | tf_op jit(solution)/shard_map/ppermute | solution.py:38
  172.5 2.6 %collective-permute-done.24 = f32[24,1280]{1,0:T(8,128)S(1)} collective-permute-done((f32[24,1280]{1,0:T(8,128)S(1)}, f32[24,1280]{1,0:T(8,128)S(1)}, u32[]{:S(2)}, u32[]{:S(2)}) %collective-permute-start.24) | collective-permute-done | bytes 122912 | tf_op jit(solution)/shard_map/ppermute | solution.py:38
  175.1 3.6 %collective-permute-start.25 = (f32[24,2560]{1,0:T(8,128)S(1)}, f32[24,2560]{1,0:T(8,128)S(1)}, u32[]{:S(2)}, u32[]{:S(2)}) collective-permute-start(f32[24,2560]{1,0:T(8,128)S(1)} %pad_maximum_fusion.1), channel_id=1, source_target_pairs={{0,384},{16,400},{32,416},{48,432},{64,448},{80,464},{96,480},{112... | collective-permute-start | bytes 737288 | tf_op jit(solution)/shard_map/ppermute | solution.py:38
  180.6 4.6 %collective-permute-start.23 = (bf16[160,2560]{1,0:T(8,128)(2,1)S(1)}, bf16[160,2560]{1,0:T(8,128)(2,1)S(1)}, u32[]{:S(2)}, u32[]{:S(2)}) collective-permute-start(bf16[160,2560]{1,0:T(8,128)(2,1)S(1)} %collective-permute-done.19.refs_10_), channel_id=1, source_target_pairs={{0,14},{16,30},{32,46},{48,62},{64,78},{80,94},{96,110},{112,126},... | collective-permute-start | bytes 2457608 | tf_op jit(solution)/shard_map/ppermute | solution.py:38
  185.3 12.3 %collective-permute-done.22.refs_9_ = bf16[160,2560]{1,0:T(8,128)(2,1)S(1)} collective-permute-done((bf16[160,2560]{1,0:T(8,128)(2,1)S(1)}, bf16[160,2560]{1,0:T(8,128)(2,1)S(1)}, u32[]{:S(2)}, u32[]{:S(2)}) %collective-permute-start.22) | collective-permute-done | bytes 819232 | tf_op jit(solution)/shard_map/ppermute | solution.py:38
  198.5 7.0 %collective-permute-start.28 = (f32[24,5120]{1,0:T(8,128)S(1)}, f32[24,5120]{1,0:T(8,128)S(1)}, u32[]{:S(2)}, u32[]{:S(2)}) collective-permute-start(f32[24,5120]{1,0:T(8,128)S(1)} %pad_maximum_fusion), channel_id=1, source_target_pairs={{0,16},{16,0},{32,48},{48,32},{64,80},{80,64},{96,112},{112,96},{1... | collective-permute-start | bytes 1474568 | tf_op jit(solution)/shard_map/ppermute | solution.py:38
  207.6 5.2 %collective-permute-start.27 = (bf16[160,2560]{1,0:T(8,128)(2,1)S(1)}, bf16[160,2560]{1,0:T(8,128)(2,1)S(1)}, u32[]{:S(2)}, u32[]{:S(2)}) collective-permute-start(bf16[160,2560]{1,0:T(8,128)(2,1)S(1)} %collective-permute-done.23.refs_11_), channel_id=1, source_target_pairs={{0,14},{16,30},{32,46},{48,62},{64,78},{80,94},{96,110},{112,126},... | collective-permute-start | bytes 2457608 | tf_op jit(solution)/shard_map/ppermute | solution.py:38
  212.8 5.4 %shard_map.86.refs_4_ = f32[256,2560]{1,0:T(8,128)S(1)} custom-call(s32[16]{0:T(128)S(1)} %pad_add_fusion.slots_ref, bf16[16,256,160]{2,1,0:T(8,128)(2,1)S(1)} %bitcast.30, bf16[16,256,160]{2,1,0:T(8,128)(2,1)S(1)} %bitcast.31, bf16[16,256,160]{2,1,0:T(8,128)(2,1)S(1)} %bitcast.32, bf16[16,256,160]{2,1,0:T(8,128)(2,1)S(1)} %bitcast.33, ...), custom_call_target="tpu_custom_call" | custom-call | flops 1258291200 | bytes 8847360 | tf_op jit(solution)/shard_map/pallas_call | solution.py:63
  220.9 8.5 %collective-permute-done.26.refs_2_ = bf16[160,2560]{1,0:T(8,128)(2,1)S(1)} collective-permute-done((bf16[160,2560]{1,0:T(8,128)(2,1)S(1)}, bf16[160,2560]{1,0:T(8,128)(2,1)S(1)}, u32[]{:S(2)}, u32[]{:S(2)}) %collective-permute-start.26) | collective-permute-done | bytes 819232 | tf_op jit(solution)/shard_map/ppermute | solution.py:38
  230.5 3.7 %shard_map.87 = bf16[256,2560]{1,0:T(8,128)(2,1)} custom-call(s32[16]{0:T(128)S(1)} %pad_add_fusion.slots_ref, bf16[16,256,160]{2,1,0:T(8,128)(2,1)S(1)} %bitcast.36, bf16[16,256,160]{2,1,0:T(8,128)(2,1)S(1)} %bitcast.37, bf16[160,2560]{1,0:T(8,128)(2,1)S(1)} %collective-permute-done.26.refs_2_, bf16[160,2560]{1,0:T(8,128)(2,1)S(1)} %collective-permute-done.27.refs_3_, ...), custom_call_target="tpu_custom_call" | custom-call | flops 419430400 | bytes 5570560 | tf_op jit(solution)/shard_map/pallas_call | solution.py:63
  (74 shorter events, 41.6 us)
Async XLA Ops:
  0.6 52.9 %collective-permute-start.1 = (bf16[160,2560]{1,0:T(8,128)(2,1)}, bf16[160,2560]{1,0:T(8,128)(2,1)S(1)}, u32[]{:S(2)}, u32[]{:S(2)}) collective-permute-start(bf16[160,2560]{1,0:T(8,128)(2,1)} %bitcast.38), channel_id=1, source_target_pairs={{0,14},{16,30},{32,46},{48,62},{64,78},{80,94},{96,110},{112,126},... | collective-permute-start | bytes 2457608 | tf_op jit(solution)/shard_map/ppermute | solution.py:38
  6.6 47.0 %collective-permute-start = (bf16[160,2560]{1,0:T(8,128)(2,1)}, bf16[160,2560]{1,0:T(8,128)(2,1)S(1)}, u32[]{:S(2)}, u32[]{:S(2)}) collective-permute-start(bf16[160,2560]{1,0:T(8,128)(2,1)} %bitcast.39), channel_id=1, source_target_pairs={{0,2},{16,18},{32,34},{48,50},{64,66},{80,82},{96,98},{112,114},{1... | collective-permute-start | bytes 2457608 | tf_op jit(solution)/shard_map/ppermute | solution.py:38
  9.8 12.3 %copy-start = (bf16[1,160,2560]{2,1,0:T(8,128)(2,1)S(1)}, bf16[1,160,2560]{2,1,0:T(8,128)(2,1)}, u32[]{:S(2)}) copy-start(bf16[1,160,2560]{2,1,0:T(8,128)(2,1)} %param.7) | copy-start | bytes 2457604
  11.6 20.1 %collective-permute-start.4 = (bf16[24,5120]{1,0:T(8,128)(2,1)S(1)}, bf16[24,5120]{1,0:T(8,128)(2,1)}, u32[]{:S(2)}, u32[]{:S(2)}) collective-permute-start(bf16[24,5120]{1,0:T(8,128)(2,1)S(1)} %broadcast_select_fusion.2), channel_id=1, source_target_pairs={{0,16},{16,0},{32,48},{48,32},{64,80},{80,64},{96,112},{112,96},{1... | collective-permute-start | bytes 737288 | tf_op jit(solution)/shard_map/ppermute | solution.py:38
  23.0 24.6 %collective-permute-start.3 = (bf16[80,2560]{1,0:T(8,128)(2,1)}, bf16[80,2560]{1,0:T(8,128)(2,1)}, u32[]{:S(2)}, u32[]{:S(2)}) collective-permute-start(bf16[80,2560]{1,0:T(8,128)(2,1)} %get-tuple-element.73), channel_id=1, source_target_pairs={{0,129},{16,145},{32,161},{48,177},{64,0},{80,16},{96,32},{112,48}... | collective-permute-start | bytes 1228808 | tf_op jit(solution)/shard_map/ppermute | solution.py:38
  29.7 23.8 %collective-permute-start.2 = (bf16[80,2560]{1,0:T(8,128)(2,1)}, bf16[80,2560]{1,0:T(8,128)(2,1)}, u32[]{:S(2)}, u32[]{:S(2)}) collective-permute-start(bf16[80,2560]{1,0:T(8,128)(2,1)} %get-tuple-element.74), channel_id=1, source_target_pairs={{0,64},{16,80},{32,96},{48,112},{64,128},{80,144},{96,160},{112,17... | collective-permute-start | bytes 1228808 | tf_op jit(solution)/shard_map/ppermute | solution.py:38
  53.5 66.5 %copy-start.1 = (bf16[160,2560]{1,0:T(8,128)(2,1)}, bf16[160,2560]{1,0:T(8,128)(2,1)S(1)}, u32[]{:S(2)}) copy-start(bf16[160,2560]{1,0:T(8,128)(2,1)S(1)} %collective-permute-done.1.refs_10_) | copy-start | bytes 2457604
  53.5 66.5 %copy-start.3 = (bf16[160,2560]{1,0:T(8,128)(2,1)}, bf16[160,2560]{1,0:T(8,128)(2,1)S(1)}, u32[]{:S(2)}) copy-start(bf16[160,2560]{1,0:T(8,128)(2,1)S(1)} %collective-permute-done.refs_9_) | copy-start | bytes 2457604
  53.6 18.9 %collective-permute-start.9 = (f32[24,2560]{1,0:T(8,128)S(1)}, f32[24,2560]{1,0:T(8,128)S(1)}, u32[]{:S(2)}, u32[]{:S(2)}) collective-permute-start(f32[24,2560]{1,0:T(8,128)S(1)} %slice_select_fusion), channel_id=1, source_target_pairs={{0,384},{16,400},{32,416},{48,432},{64,448},{80,464},{96,480},{112... | collective-permute-start | bytes 737288 | tf_op jit(solution)/shard_map/ppermute | solution.py:38
  58.2 31.9 %collective-permute-start.5 = (bf16[160,2560]{1,0:T(8,128)(2,1)S(1)}, bf16[160,2560]{1,0:T(8,128)(2,1)}, u32[]{:S(2)}, u32[]{:S(2)}) collective-permute-start(bf16[160,2560]{1,0:T(8,128)(2,1)S(1)} %collective-permute-done.refs_9_), channel_id=1, source_target_pairs={{0,2},{16,18},{32,34},{48,50},{64,66},{80,82},{96,98},{112,114},{1... | collective-permute-start | bytes 2457608 | tf_op jit(solution)/shard_map/ppermute | solution.py:38
  60.2 29.9 %collective-permute-start.6 = (bf16[160,2560]{1,0:T(8,128)(2,1)S(1)}, bf16[160,2560]{1,0:T(8,128)(2,1)}, u32[]{:S(2)}, u32[]{:S(2)}) collective-permute-start(bf16[160,2560]{1,0:T(8,128)(2,1)S(1)} %collective-permute-done.1.refs_10_), channel_id=1, source_target_pairs={{0,14},{16,30},{32,46},{48,62},{64,78},{80,94},{96,110},{112,126},... | collective-permute-start | bytes 2457608 | tf_op jit(solution)/shard_map/ppermute | solution.py:38
  65.0 22.8 %collective-permute-start.7 = (bf16[80,2560]{1,0:T(8,128)(2,1)}, bf16[80,2560]{1,0:T(8,128)(2,1)S(1)}, u32[]{:S(2)}, u32[]{:S(2)}) collective-permute-start(bf16[80,2560]{1,0:T(8,128)(2,1)} %collective-permute-done.2), channel_id=1, source_target_pairs={{0,64},{16,80},{32,96},{48,112},{64,128},{80,144},{96,160},{112,17... | collective-permute-start | bytes 1228808 | tf_op jit(solution)/shard_map/ppermute | solution.py:38
  67.0 23.1 %collective-permute-start.8 = (bf16[80,2560]{1,0:T(8,128)(2,1)}, bf16[80,2560]{1,0:T(8,128)(2,1)S(1)}, u32[]{:S(2)}, u32[]{:S(2)}) collective-permute-start(bf16[80,2560]{1,0:T(8,128)(2,1)} %collective-permute-done.3), channel_id=1, source_target_pairs={{0,129},{16,145},{32,161},{48,177},{64,0},{80,16},{96,32},{112,48}... | collective-permute-start | bytes 1228808 | tf_op jit(solution)/shard_map/ppermute | solution.py:38
  90.1 27.4 %collective-permute-start.10 = (bf16[160,2560]{1,0:T(8,128)(2,1)}, bf16[160,2560]{1,0:T(8,128)(2,1)}, u32[]{:S(2)}, u32[]{:S(2)}) collective-permute-start(bf16[160,2560]{1,0:T(8,128)(2,1)} %collective-permute-done.5.refs_11_), channel_id=1, source_target_pairs={{0,2},{16,18},{32,34},{48,50},{64,66},{80,82},{96,98},{112,114},{1... | collective-permute-start | bytes 2457608 | tf_op jit(solution)/shard_map/ppermute | solution.py:38
  92.0 25.5 %collective-permute-start.11 = (bf16[160,2560]{1,0:T(8,128)(2,1)}, bf16[160,2560]{1,0:T(8,128)(2,1)S(1)}, u32[]{:S(2)}, u32[]{:S(2)}) collective-permute-start(bf16[160,2560]{1,0:T(8,128)(2,1)} %collective-permute-done.6.refs_12_), channel_id=1, source_target_pairs={{0,14},{16,30},{32,46},{48,62},{64,78},{80,94},{96,110},{112,126},... | collective-permute-start | bytes 2457608 | tf_op jit(solution)/shard_map/ppermute | solution.py:38
  96.6 10.4 %collective-permute-start.14 = (f32[24,1280]{1,0:T(8,128)S(1)}, f32[24,1280]{1,0:T(8,128)S(1)}, u32[]{:S(2)}, u32[]{:S(2)}) collective-permute-start(f32[24,1280]{1,0:T(8,128)S(1)} %slice_select_fusion.1), channel_id=1, source_target_pairs={{0,192},{16,208},{32,224},{48,240},{64,256},{80,272},{96,288},{112... | collective-permute-start | bytes 368648 | tf_op jit(solution)/shard_map/ppermute | solution.py:38
  98.8 14.4 %collective-permute-start.12 = (bf16[80,2560]{1,0:T(8,128)(2,1)S(1)}, bf16[80,2560]{1,0:T(8,128)(2,1)S(1)}, u32[]{:S(2)}, u32[]{:S(2)}) collective-permute-start(bf16[80,2560]{1,0:T(8,128)(2,1)S(1)} %collective-permute-done.7), channel_id=1, source_target_pairs={{0,64},{16,80},{32,96},{48,112},{64,128},{80,144},{96,160},{112,17... | collective-permute-start | bytes 1228808 | tf_op jit(solution)/shard_map/ppermute | solution.py:38
  100.8 16.7 %collective-permute-start.13 = (bf16[80,2560]{1,0:T(8,128)(2,1)S(1)}, bf16[80,2560]{1,0:T(8,128)(2,1)S(1)}, u32[]{:S(2)}, u32[]{:S(2)}) collective-permute-start(bf16[80,2560]{1,0:T(8,128)(2,1)S(1)} %collective-permute-done.8), channel_id=1, source_target_pairs={{0,129},{16,145},{32,161},{48,177},{64,0},{80,16},{96,32},{112,48}... | collective-permute-start | bytes 1228808 | tf_op jit(solution)/shard_map/ppermute | solution.py:38
  120.0 18.3 %collective-permute-start.16 = (bf16[160,2560]{1,0:T(8,128)(2,1)}, bf16[160,2560]{1,0:T(8,128)(2,1)}, u32[]{:S(2)}, u32[]{:S(2)}) collective-permute-start(bf16[160,2560]{1,0:T(8,128)(2,1)} %constant_dynamic-update-slice_fusion.refs_6_), channel_id=1, source_target_pairs={{0,14},{16,30},{32,46},{48,62},{64,78},{80,94},{96,110},{112,126},... | collective-permute-start | bytes 2457608 | tf_op jit(solution)/shard_map/ppermute | solution.py:38
  122.1 19.2 %collective-permute-start.15 = (bf16[160,2560]{1,0:T(8,128)(2,1)}, bf16[160,2560]{1,0:T(8,128)(2,1)}, u32[]{:S(2)}, u32[]{:S(2)}) collective-permute-start(bf16[160,2560]{1,0:T(8,128)(2,1)} %collective-permute-done.10.refs_13_), channel_id=1, source_target_pairs={{0,2},{16,18},{32,34},{48,50},{64,66},{80,82},{96,98},{112,114},{1... | collective-permute-start | bytes 2457608 | tf_op jit(solution)/shard_map/ppermute | solution.py:38
  125.3 7.1 %collective-permute-start.17 = (f32[24,1280]{1,0:T(8,128)S(1)}, f32[24,1280]{1,0:T(8,128)S(1)}, u32[]{:S(2)}, u32[]{:S(2)}) collective-permute-start(f32[24,1280]{1,0:T(8,128)S(1)} %select_add_fusion.2), channel_id=1, source_target_pairs={{0,32},{16,48},{32,0},{48,16},{64,96},{80,112},{96,64},{112,80},{1... | collective-permute-start | bytes 368648 | tf_op jit(solution)/shard_map/ppermute | solution.py:38
  141.3 28.1 %collective-permute-start.18 = (bf16[160,2560]{1,0:T(8,128)(2,1)}, bf16[160,2560]{1,0:T(8,128)(2,1)S(1)}, u32[]{:S(2)}, u32[]{:S(2)}) collective-permute-start(bf16[160,2560]{1,0:T(8,128)(2,1)} %constant_dynamic-update-slice_fusion.refs_6_), channel_id=1, source_target_pairs={{0,2},{16,18},{32,34},{48,50},{64,66},{80,82},{96,98},{112,114},{1... | collective-permute-start | bytes 2457608 | tf_op jit(solution)/shard_map/ppermute | solution.py:38
  143.3 26.1 %collective-permute-start.19 = (bf16[160,2560]{1,0:T(8,128)(2,1)}, bf16[160,2560]{1,0:T(8,128)(2,1)S(1)}, u32[]{:S(2)}, u32[]{:S(2)}) collective-permute-start(bf16[160,2560]{1,0:T(8,128)(2,1)} %collective-permute-done.16.refs_8_), channel_id=1, source_target_pairs={{0,14},{16,30},{32,46},{48,62},{64,78},{80,94},{96,110},{112,126},... | collective-permute-start | bytes 2457608 | tf_op jit(solution)/shard_map/ppermute | solution.py:38
  147.9 21.4 %collective-permute-start.21 = (f32[24,1280]{1,0:T(8,128)S(1)}, f32[24,1280]{1,0:T(8,128)S(1)}, u32[]{:S(2)}, u32[]{:S(2)}) collective-permute-start(f32[24,1280]{1,0:T(8,128)S(1)} %add.79), channel_id=1, source_target_pairs={{0,128},{16,144},{32,160},{48,176},{64,0},{80,16},{96,32},{112,48}... | collective-permute-start | bytes 368648 | tf_op jit(solution)/shard_map/ppermute | solution.py:38
  157.6 11.8 %collective-permute-start.20 = (f32[24,1280]{1,0:T(8,128)S(1)}, f32[24,1280]{1,0:T(8,128)S(1)}, u32[]{:S(2)}, u32[]{:S(2)}) collective-permute-start(f32[24,1280]{1,0:T(8,128)S(1)} %add.79), channel_id=1, source_target_pairs={{0,64},{16,80},{32,96},{48,112},{64,128},{80,144},{96,160},{112,17... | collective-permute-start | bytes 368648 | tf_op jit(solution)/shard_map/ppermute | solution.py:38
  169.4 5.6 %collective-permute-start.24 = (f32[24,1280]{1,0:T(8,128)S(1)}, f32[24,1280]{1,0:T(8,128)S(1)}, u32[]{:S(2)}, u32[]{:S(2)}) collective-permute-start(f32[24,1280]{1,0:T(8,128)S(1)} %select_add_fusion.1), channel_id=1, source_target_pairs={{0,192},{16,208},{32,224},{48,240},{64,256},{80,272},{96,288},{112... | collective-permute-start | bytes 368648 | tf_op jit(solution)/shard_map/ppermute | solution.py:38
  175.1 10.2 %collective-permute-start.25 = (f32[24,2560]{1,0:T(8,128)S(1)}, f32[24,2560]{1,0:T(8,128)S(1)}, u32[]{:S(2)}, u32[]{:S(2)}) collective-permute-start(f32[24,2560]{1,0:T(8,128)S(1)} %pad_maximum_fusion.1), channel_id=1, source_target_pairs={{0,384},{16,400},{32,416},{48,432},{64,448},{80,464},{96,480},{112... | collective-permute-start | bytes 737288 | tf_op jit(solution)/shard_map/ppermute | solution.py:38
  178.7 18.9 %collective-permute-start.22 = (bf16[160,2560]{1,0:T(8,128)(2,1)S(1)}, bf16[160,2560]{1,0:T(8,128)(2,1)S(1)}, u32[]{:S(2)}, u32[]{:S(2)}) collective-permute-start(bf16[160,2560]{1,0:T(8,128)(2,1)S(1)} %collective-permute-done.18.refs_7_), channel_id=1, source_target_pairs={{0,2},{16,18},{32,34},{48,50},{64,66},{80,82},{96,98},{112,114},{1... | collective-permute-start | bytes 2457608 | tf_op jit(solution)/shard_map/ppermute | solution.py:38
  180.6 17.9 %collective-permute-start.23 = (bf16[160,2560]{1,0:T(8,128)(2,1)S(1)}, bf16[160,2560]{1,0:T(8,128)(2,1)S(1)}, u32[]{:S(2)}, u32[]{:S(2)}) collective-permute-start(bf16[160,2560]{1,0:T(8,128)(2,1)S(1)} %collective-permute-done.19.refs_10_), channel_id=1, source_target_pairs={{0,14},{16,30},{32,46},{48,62},{64,78},{80,94},{96,110},{112,126},... | collective-permute-start | bytes 2457608 | tf_op jit(solution)/shard_map/ppermute | solution.py:38
  198.5 19.7 %collective-permute-start.28 = (f32[24,5120]{1,0:T(8,128)S(1)}, f32[24,5120]{1,0:T(8,128)S(1)}, u32[]{:S(2)}, u32[]{:S(2)}) collective-permute-start(f32[24,5120]{1,0:T(8,128)S(1)} %pad_maximum_fusion), channel_id=1, source_target_pairs={{0,16},{16,0},{32,48},{48,32},{64,80},{80,64},{96,112},{112,96},{1... | collective-permute-start | bytes 1474568 | tf_op jit(solution)/shard_map/ppermute | solution.py:38
  205.6 23.9 %collective-permute-start.26 = (bf16[160,2560]{1,0:T(8,128)(2,1)S(1)}, bf16[160,2560]{1,0:T(8,128)(2,1)S(1)}, u32[]{:S(2)}, u32[]{:S(2)}) collective-permute-start(bf16[160,2560]{1,0:T(8,128)(2,1)S(1)} %collective-permute-done.22.refs_9_), channel_id=1, source_target_pairs={{0,2},{16,18},{32,34},{48,50},{64,66},{80,82},{96,98},{112,114},{1... | collective-permute-start | bytes 2457608 | tf_op jit(solution)/shard_map/ppermute | solution.py:38
  207.6 23.0 %collective-permute-start.27 = (bf16[160,2560]{1,0:T(8,128)(2,1)S(1)}, bf16[160,2560]{1,0:T(8,128)(2,1)S(1)}, u32[]{:S(2)}, u32[]{:S(2)}) collective-permute-start(bf16[160,2560]{1,0:T(8,128)(2,1)S(1)} %collective-permute-done.23.refs_11_), channel_id=1, source_target_pairs={{0,14},{16,30},{32,46},{48,62},{64,78},{80,94},{96,110},{112,126},... | collective-permute-start | bytes 2457608 | tf_op jit(solution)/shard_map/ppermute | solution.py:38
  (6 other events, 6.7 us)

commit v2 on v1

v2 whole, which is shorter than its diff:
```python
import jax
import jax.numpy as jnp
from jax import lax
from jax.experimental import pallas as pl
from jax.experimental.pallas import tpu as pltpu
from jax.sharding import PartitionSpec as P

Y, ZH, ZL, X, C = 8, 2, 6, 4, 2


def moved(to):
    def place(x, y, z, c):
        return (((x * ZL + z % ZL) * C + c) * Y + y) * ZH + z // ZL

    return [
        (place(x, y, z, c), place(*to(x, y, z, c)))
        for x in range(X)
        for y in range(Y)
        for z in range(ZL * ZH)
        for c in range(C)
    ]


UP = moved(lambda x, y, z, c: (x, (y + 1) % Y, z, c))
DOWN = moved(lambda x, y, z, c: (x, (y - 1) % Y, z, c))
CROSS = moved(lambda x, y, z, c: (x, y, (z + ZL) % (ZL * ZH), c))
CORE = moved(lambda x, y, z, c: (x, y, z, 1 - c))
X_FAR = moved(lambda x, y, z, c: (x ^ 2, y, z, c))
X_NEAR = moved(lambda x, y, z, c: (x ^ 1, y, z, c))
Z_PAIR = moved(lambda x, y, z, c: (x, y, z ^ 1, c))
Z_TWO = moved(lambda x, y, z, c: (x, y, (z // ZL) * ZL + (z % ZL + 2) % ZL, c))
Z_FOUR = moved(lambda x, y, z, c: (x, y, (z // ZL) * ZL + (z % ZL + 4) % ZL, c))


def send_to(array, pairs):
    return lax.ppermute(array, ("rep", "fsdp"), pairs)


def product(slot, tokens, weights, total, out_dtype):
    rows, depth = tokens.shape[1:]
    width = weights.shape[1]
    tile = width // 2

    def kernel(slot_ref, *refs):
        del slot_ref
        acc = jnp.dot(refs[0][0], refs[1][...], preferred_element_type=jnp.float32)
        if total is not None:
            acc += refs[2][...]
        refs[-1][...] = acc.astype(out_dtype)

    in_specs = [
        pl.BlockSpec((1, rows, depth), lambda j, at: (at[0], 0, 0)),
        pl.BlockSpec((depth, tile), lambda j, at: (0, j)),
    ]
    operands = [slot, tokens, weights]
    if total is not None:
        in_specs.append(pl.BlockSpec((rows, tile), lambda j, at: (0, j)))
        operands.append(total)
    return pl.pallas_call(
        kernel,
        grid_spec=pltpu.PrefetchScalarGridSpec(
            num_scalar_prefetch=1,
            grid=(width // tile,),
            in_specs=in_specs,
            out_specs=pl.BlockSpec((rows, tile), lambda j, at: (0, j)),
        ),
        out_shape=jax.ShapeDtypeStruct((rows, width), out_dtype),
        compiler_params=pltpu.CompilerParams(vmem_limit_bytes=56 << 20),
        cost_estimate=pl.CostEstimate(
            flops=2 * rows * width * depth,
            bytes_accessed=2 * width * depth + 6 * rows * width,
            transcendentals=0,
        ),
    )(*operands)


def fragment_term(base_wide, local_frag, block_exps):
    exps = block_exps.astype(jnp.float32)
    scale = jnp.repeat(jnp.exp2(exps), 128, axis=1)
    inverse = jnp.repeat(jnp.exp2(-exps), 128, axis=1)
    level = jnp.clip((base_wide - local_frag.astype(jnp.float32)) * inverse, -1.0, 1.0)
    return level.astype(jnp.bfloat16) * scale.astype(jnp.bfloat16)


def keep_and_send(array, index, axis):
    half = array.shape[axis] // 2
    first = lax.slice_in_dim(array, 0, half, axis=axis)
    second = lax.slice_in_dim(array, half, 2 * half, axis=axis)
    return jnp.where(index == 0, first, second), jnp.where(index == 0, second, first)


def join(mine, other, index, axis):
    return jnp.concatenate(
        [jnp.where(index == 0, mine, other), jnp.where(index == 0, other, mine)], axis=axis
    )


def together(*arrays):
    return lax.optimization_barrier(arrays)


def gather_y(array):
    groups = [[y * ZH + h for y in range(Y)] for h in range(ZH)]
    return lax.all_gather(array, "fsdp", axis=0, tiled=True, axis_index_groups=groups)


def per_device(attn_heads, proj_weight, base_frag, local_frag, block_exps, momentum):
    own = proj_weight[0]
    h = lax.axis_index("fsdp") % ZH
    index = lax.axis_index("rep")
    core, z, x = index % C, (index // C) % ZL, index // (C * ZL)
    far, near, third = x // 2, x % 2, z // 2
    base_wide = base_frag.astype(jnp.float32)

    gathered = gather_y(own)
    other = send_to(own, CROSS)
    keep, give = keep_and_send(fragment_term(base_wide, local_frag[0], block_exps[0]), core, 0)
    part = keep.astype(jnp.float32) + send_to(give, CORE).astype(jnp.float32)
    keep, give = keep_and_send(part, far, 1)
    part = keep + send_to(give, X_FAR)
    rows, width = attn_heads.shape
    tokens = attn_heads.reshape(rows, Y, ZH, width // (Y * ZH)).transpose(2, 0, 1, 3)
    tokens = tokens.reshape(ZH, rows, width // ZH)
    other, part, tokens = together(other, part, tokens)

    over_gathered = gather_y(other)
    keep, give = keep_and_send(part, near, 1)
    part = keep + send_to(give, X_NEAR)
    total = product(h[None].astype(jnp.int32), tokens, gathered, None, jnp.float32)
    part = part + send_to(part, Z_PAIR)
    part, total = together(part, total)
    two, four = send_to(part, Z_TWO), send_to(part, Z_FOUR)
    zero = jnp.where(third == 0, part, jnp.where(third == 1, two, four))
    one = jnp.where(third == 1, part, jnp.where(third == 2, two, four))
    last = jnp.where(third == 2, part, jnp.where(third == 0, two, four))
    part = (zero + one) + last
    part = join(part, send_to(part, X_NEAR), near, 1)
    part = join(part, send_to(part, X_FAR), far, 1)
    outer_grad = join(part, send_to(part, CORE), core, 0) / (X * ZL * C)
    new_momentum = 0.9 * momentum + outer_grad
    new_base = (base_wide - 0.7 * (outer_grad + 0.9 * new_momentum)).astype(jnp.bfloat16)

    total, new_momentum, new_base = together(total, new_momentum, new_base)
    mixed = product((1 - h)[None].astype(jnp.int32), tokens, over_gathered, total, jnp.bfloat16)
    return mixed, new_base, new_momentum


def solution(mesh):
    return jax.shard_map(
        per_device,
        mesh=mesh,
        in_specs=(
            P(("rep", "fsdp"), None),
            P("rep", "fsdp", None),
            P("fsdp", None),
            P("rep", "fsdp", None),
            P("rep", "fsdp", None),
            P("fsdp", None),
        ),
        out_specs=(P(("rep", "fsdp"), None), P("fsdp", None), P("fsdp", None)),
        check_vma=False,
    )
```

time: 236 us -> 196 us (0.83)
  starting transfers between devices: 115 us -> 81.8 us
  between operations: 1.28 us -> 14.4 us
  local copies, waits for them, and re-layouts: 14 us -> 4.03 us
  Pallas kernels: 15.5 us -> 10.9 us
    ppermute x29 -> x10, waiting for transfers between devices: 83.1 us -> 45.2 us  [send_to(): return lax.ppermute(array, ('rep', 'fsdp'), pairs)]
    all_gather x0 -> x2, waiting for transfers between devices: none -> 35.1 us  [gather_y(): lax.all_gather(array, 'fsdp', axis=0, tiled=True, axis_index_groups=groups)]
    ppermute x29 -> x10, starting transfers between devices: 115 us -> 81.7 us  [send_to(): return lax.ppermute(array, ('rep', 'fsdp'), pairs)]
    unnamed x19 -> x9, local copies, waits for them, and re-layouts: 6.4 us -> 1.67 us
    pallas_call x3 -> x2, Pallas kernels: 15.5 us -> 10.9 us  [product(): pl.pallas_call(kernel, grid_spec=pltpu.PrefetchScalarGridSpec(num_scalar_...]
    reshape x1 -> x0, local copies, waits for them, and re-layouts: 2.68 us -> none  [per_device(): tokens = heads.reshape(rows, Y * ZH, 2 * HALF).transpose(1, 0, 2)]
  transfers between devices with their start and end apart: 29 -> 12, of which waited for: 13 -> 10; matrix products, arithmetic and copies ran while one was open for 5% -> 4% of each run, Pallas kernels for 5% -> 3%
where the time goes in v2:
time: 196 us
  starting transfers between devices  81.8 us (42%)
  waiting for transfers between devices  80.9 us (41%)
  between operations  14.4 us (7%)
  Pallas kernels  10.9 us (6%)
  local copies, waits for them, and re-layouts  4.03 us (2%)
  other arithmetic  3.84 us (2%)
    ppermute x10, starting transfers between devices, send_to(): return lax.ppermute(array, ('rep', 'fsdp'), pairs)  81.7 us
    ppermute x10, waiting for transfers between devices, send_to(): return lax.ppermute(array, ('rep', 'fsdp'), pairs)  45.2 us
    all_gather x2, waiting for transfers between devices, gather_y(): lax.all_gather(array, 'fsdp', axis=0, tiled=True, axis_index_groups=groups)  35.1 us
    pallas_call x2, Pallas kernels, product(): pl.pallas_call(kernel, grid_spec=pltpu.PrefetchScalarGridSpec(num_scalar_...  10.9 us
  transfers between devices with their start and end apart: 12, of which 10 were waited for; matrix products, arithmetic and copies ran while one was open for 4% of the time, Pallas kernels for 3%

profile of v2, /device:TPU:1, one launch (start us, length us, event | category | flops | bytes accessed | tf_op | source)
XLA Modules:
  0.0 196.0 jit_solution(6627199606703488580)
XLA Ops:
  7.2 0.7 all-gather.6.cloned.1.call-update
  8.0 0.7 fusion.5
  8.7 0.1 copy.13
  8.9 0.3 broadcast_in_dim.14
  9.2 0.3 broadcast_in_dim.13
  9.6 0.3 fusion.4
  9.9 12.4 %collective-permute-start.1 = (bf16[24,5120]{1,0:T(8,128)(2,1)S(1)}, bf16[24,5120]{1,0:T(8,128)(2,1)S(1)}, u32[]{:S(2)}, u32[]{:S(2)}) collective-permute-start(bf16[24,5120]{1,0:T(8,128)(2,1)S(1)} %broadcast_select_fusion.2), channel_id=1, source_target_pairs={{0,16},{16,0},{32,48},{48,32},{64,80},{80,64},{96,112},{112,96},{1... | collective-permute-start | bytes 737288 | tf_op jit(solution)/shard_map/ppermute | solution.py:36
  22.4 1.1 collective-permute-done.1
  23.6 1.9 collective-permute-start.2
  25.5 8.6 %collective-permute-start = (bf16[160,2560]{1,0:T(8,128)(2,1)}, bf16[160,2560]{1,0:T(8,128)(2,1)}, u32[]{:S(2)}, u32[]{:S(2)}) collective-permute-start(bf16[160,2560]{1,0:T(8,128)(2,1)} %bitcast.1), channel_id=1, source_target_pairs={{0,1},{16,17},{32,33},{48,49},{64,65},{80,81},{96,97},{112,113},{1... | collective-permute-start | bytes 2457608 | tf_op jit(solution)/shard_map/ppermute | solution.py:36
  34.1 1.6 copy.14
  35.9 1.0 select_add_fusion
  36.8 20.0 %collective-permute-done = bf16[160,2560]{1,0:T(8,128)(2,1)} collective-permute-done((bf16[160,2560]{1,0:T(8,128)(2,1)}, bf16[160,2560]{1,0:T(8,128)(2,1)}, u32[]{:S(2)}, u32[]{:S(2)}) %collective-permute-start) | collective-permute-done | bytes 819232 | tf_op jit(solution)/shard_map/ppermute | solution.py:36
  57.0 1.9 collective-permute-start.3
  58.9 4.1 %collective-permute-done.3 = f32[24,1280]{1,0:T(8,128)S(1)} collective-permute-done((f32[24,1280]{1,0:T(8,128)S(1)}, f32[24,1280]{1,0:T(8,128)S(1)}, u32[]{:S(2)}, u32[]{:S(2)}) %collective-permute-start.3) | collective-permute-done | bytes 122912 | tf_op jit(solution)/shard_map/ppermute | solution.py:36
  63.0 33.9 %collective-permute-start.4 = (f32[24,1280]{1,0:T(8,128)S(1)}, f32[24,1280]{1,0:T(8,128)S(1)}, u32[]{:S(2)}, u32[]{:S(2)}) collective-permute-start(f32[24,1280]{1,0:T(8,128)S(1)} %select_add_fusion.2), channel_id=1, source_target_pairs={{0,32},{16,48},{32,0},{48,16},{64,96},{80,112},{96,64},{112,80},{1... | collective-permute-start | bytes 368648 | tf_op jit(solution)/shard_map/ppermute | solution.py:36
  97.0 1.5 copy.17.refs_0_
  98.4 1.2 collective-permute-done.4
  99.6 0.3 all-gather.6.cloned.1.call-done
  100.0 5.3 %shard_map.85.refs_2_ = f32[256,2560]{1,0:T(8,128)} custom-call(s32[1]{0:T(128)} %bitcast.8.slot_ref, bf16[2,256,1280]{2,1,0:T(8,128)(2,1)} %copy.17.refs_0_, bf16[1280,2560]{1,0:T(8,128)(2,1)} %bitcast.23), custom_call_target="tpu_custom_call" | custom-call | flops 1677721600 | bytes 10485760 | tf_op jit(solution)/shard_map/pallas_call | solution.py:59
  105.2 7.7 %collective-permute-start.6 = (f32[24,1280]{1,0:T(8,128)S(1)}, f32[24,1280]{1,0:T(8,128)S(1)}, u32[]{:S(2)}, u32[]{:S(2)}) collective-permute-start(f32[24,1280]{1,0:T(8,128)S(1)} %add.47), channel_id=1, source_target_pairs={{0,128},{16,144},{32,160},{48,176},{64,0},{80,16},{96,32},{112,48}... | collective-permute-start | bytes 368648 | tf_op jit(solution)/shard_map/ppermute | solution.py:36
  113.0 1.9 collective-permute-start.5
  114.9 10.5 %collective-permute-done.5 = f32[24,1280]{1,0:T(8,128)S(1)} collective-permute-done((f32[24,1280]{1,0:T(8,128)S(1)}, f32[24,1280]{1,0:T(8,128)S(1)}, u32[]{:S(2)}, u32[]{:S(2)}) %collective-permute-start.5) | collective-permute-done | bytes 122912 | tf_op jit(solution)/shard_map/ppermute | solution.py:36
  125.5 3.1 %collective-permute-start.7 = (f32[24,1280]{1,0:T(8,128)S(1)}, f32[24,1280]{1,0:T(8,128)S(1)}, u32[]{:S(2)}, u32[]{:S(2)}) collective-permute-start(f32[24,1280]{1,0:T(8,128)S(1)} %select_add_fusion.1), channel_id=1, source_target_pairs={{0,192},{16,208},{32,224},{48,240},{64,256},{80,272},{96,288},{112... | collective-permute-start | bytes 368648 | tf_op jit(solution)/shard_map/ppermute | solution.py:36
  128.6 2.9 %collective-permute-done.7 = f32[24,1280]{1,0:T(8,128)S(1)} collective-permute-done((f32[24,1280]{1,0:T(8,128)S(1)}, f32[24,1280]{1,0:T(8,128)S(1)}, u32[]{:S(2)}, u32[]{:S(2)}) %collective-permute-start.7) | collective-permute-done | bytes 122912 | tf_op jit(solution)/shard_map/ppermute | solution.py:36
  131.6 4.6 %collective-permute-start.8 = (f32[24,2560]{1,0:T(8,128)S(1)}, f32[24,2560]{1,0:T(8,128)S(1)}, u32[]{:S(2)}, u32[]{:S(2)}) collective-permute-start(f32[24,2560]{1,0:T(8,128)S(1)} %pad_maximum_fusion.1), channel_id=1, source_target_pairs={{0,384},{16,400},{32,416},{48,432},{64,448},{80,464},{96,480},{112... | collective-permute-start | bytes 737288 | tf_op jit(solution)/shard_map/ppermute | solution.py:36
  136.2 3.9 %collective-permute-done.8 = f32[24,2560]{1,0:T(8,128)S(1)} collective-permute-done((f32[24,2560]{1,0:T(8,128)S(1)}, f32[24,2560]{1,0:T(8,128)S(1)}, u32[]{:S(2)}, u32[]{:S(2)}) %collective-permute-start.8) | collective-permute-done | bytes 245792 | tf_op jit(solution)/shard_map/ppermute | solution.py:36
  140.2 5.5 %collective-permute-start.9 = (f32[24,5120]{1,0:T(8,128)S(1)}, f32[24,5120]{1,0:T(8,128)S(1)}, u32[]{:S(2)}, u32[]{:S(2)}) collective-permute-start(f32[24,5120]{1,0:T(8,128)S(1)} %pad_maximum_fusion), channel_id=1, source_target_pairs={{0,16},{16,0},{32,48},{48,32},{64,80},{80,64},{96,112},{112,96},{1... | collective-permute-start | bytes 1474568 | tf_op jit(solution)/shard_map/ppermute | solution.py:36
  145.8 1.5 collective-permute-done.9
  147.3 1.4 fusion.3
  148.7 34.7 %all-gather.4.cloned.1.call-done.refs_1_ = bf16[1280,2560]{1,0:T(8,128)(2,1)} async-done(((bf16[160,2560]{1,0:T(8,128)(2,1)}), bf16[1280,2560]{1,0:T(8,128)(2,1)}) %all-gather.4.cloned.1.call-update) | async-done | bytes 6553616 | tf_op jit(solution)/shard_map/all_gather | solution.py:104
  183.4 5.7 %shard_map.86 = bf16[256,2560]{1,0:T(8,128)(2,1)} custom-call(s32[1]{0:T(128)} %bitcast.slot_ref, bf16[2,256,1280]{2,1,0:T(8,128)(2,1)} %copy.17.refs_0_, bf16[1280,2560]{1,0:T(8,128)(2,1)} %all-gather.4.cloned.1.call-done.refs_1_, f32[256,2560]{1,0:T(8,128)} %shard_map.85.refs_2_), custom_call_target="tpu_custom_call" | custom-call | flops 1677721600 | bytes 10485760 | tf_op jit(solution)/shard_map/pallas_call | solution.py:59
  (27 shorter events, 0.7 us)
Async XLA Ops:
  7.2 2.4 %copy-start = (bf16[48,5120]{1,0:T(8,128)(2,1)S(1)}, bf16[48,5120]{1,0:T(8,128)(2,1)}, u32[]{:S(2)}) copy-start(bf16[48,5120]{1,0:T(8,128)(2,1)} %param.8) | copy-start | bytes 1474564
  7.2 2.4 %copy-start.3 = (bf16[1,48,5120]{2,1,0:T(8,128)(2,1)S(1)}, bf16[1,48,5120]{2,1,0:T(8,128)(2,1)}, u32[]{:S(2)}) copy-start(bf16[1,48,5120]{2,1,0:T(8,128)(2,1)} %param.9) | copy-start | bytes 1474564
  7.2 92.8 %all-gather.6.cloned.1.call-start = ((), (), s32[]{:S(2)}) async-start(), calls=%async_computation.1 | async-start | bytes 7372800 | tf_op jit(solution)/shard_map/all_gather | solution.py:104
  7.9 175.5 %all-gather.4.cloned.1.call-start = ((), (), s32[]{:S(2)}) async-start(), calls=%async_computation | async-start | bytes 7372800 | tf_op jit(solution)/shard_map/all_gather | solution.py:104
  9.9 13.5 %collective-permute-start.1 = (bf16[24,5120]{1,0:T(8,128)(2,1)S(1)}, bf16[24,5120]{1,0:T(8,128)(2,1)S(1)}, u32[]{:S(2)}, u32[]{:S(2)}) collective-permute-start(bf16[24,5120]{1,0:T(8,128)(2,1)S(1)} %broadcast_select_fusion.2), channel_id=1, source_target_pairs={{0,16},{16,0},{32,48},{48,32},{64,80},{80,64},{96,112},{112,96},{1... | collective-permute-start | bytes 737288 | tf_op jit(solution)/shard_map/ppermute | solution.py:36
  23.6 12.3 %collective-permute-start.2 = (f32[24,2560]{1,0:T(8,128)S(1)}, f32[24,2560]{1,0:T(8,128)}, u32[]{:S(2)}, u32[]{:S(2)}) collective-permute-start(f32[24,2560]{1,0:T(8,128)S(1)} %slice_select_fusion), channel_id=1, source_target_pairs={{0,384},{16,400},{32,416},{48,432},{64,448},{80,464},{96,480},{112... | collective-permute-start | bytes 737288 | tf_op jit(solution)/shard_map/ppermute | solution.py:36
  25.5 31.4 %collective-permute-start = (bf16[160,2560]{1,0:T(8,128)(2,1)}, bf16[160,2560]{1,0:T(8,128)(2,1)}, u32[]{:S(2)}, u32[]{:S(2)}) collective-permute-start(bf16[160,2560]{1,0:T(8,128)(2,1)} %bitcast.1), channel_id=1, source_target_pairs={{0,1},{16,17},{32,33},{48,49},{64,65},{80,81},{96,97},{112,113},{1... | collective-permute-start | bytes 2457608 | tf_op jit(solution)/shard_map/ppermute | solution.py:36
  57.0 6.0 %collective-permute-start.3 = (f32[24,1280]{1,0:T(8,128)S(1)}, f32[24,1280]{1,0:T(8,128)S(1)}, u32[]{:S(2)}, u32[]{:S(2)}) collective-permute-start(f32[24,1280]{1,0:T(8,128)S(1)} %slice_select_fusion.1), channel_id=1, source_target_pairs={{0,192},{16,208},{32,224},{48,240},{64,256},{80,272},{96,288},{112... | collective-permute-start | bytes 368648 | tf_op jit(solution)/shard_map/ppermute | solution.py:36
  63.0 36.6 %collective-permute-start.4 = (f32[24,1280]{1,0:T(8,128)S(1)}, f32[24,1280]{1,0:T(8,128)S(1)}, u32[]{:S(2)}, u32[]{:S(2)}) collective-permute-start(f32[24,1280]{1,0:T(8,128)S(1)} %select_add_fusion.2), channel_id=1, source_target_pairs={{0,32},{16,48},{32,0},{48,16},{64,96},{80,112},{96,64},{112,80},{1... | collective-permute-start | bytes 368648 | tf_op jit(solution)/shard_map/ppermute | solution.py:36
  105.2 9.7 %collective-permute-start.6 = (f32[24,1280]{1,0:T(8,128)S(1)}, f32[24,1280]{1,0:T(8,128)S(1)}, u32[]{:S(2)}, u32[]{:S(2)}) collective-permute-start(f32[24,1280]{1,0:T(8,128)S(1)} %add.47), channel_id=1, source_target_pairs={{0,128},{16,144},{32,160},{48,176},{64,0},{80,16},{96,32},{112,48}... | collective-permute-start | bytes 368648 | tf_op jit(solution)/shard_map/ppermute | solution.py:36
  113.0 12.5 %collective-permute-start.5 = (f32[24,1280]{1,0:T(8,128)S(1)}, f32[24,1280]{1,0:T(8,128)S(1)}, u32[]{:S(2)}, u32[]{:S(2)}) collective-permute-start(f32[24,1280]{1,0:T(8,128)S(1)} %add.47), channel_id=1, source_target_pairs={{0,64},{16,80},{32,96},{48,112},{64,128},{80,144},{96,160},{112,17... | collective-permute-start | bytes 368648 | tf_op jit(solution)/shard_map/ppermute | solution.py:36
  125.5 6.0 %collective-permute-start.7 = (f32[24,1280]{1,0:T(8,128)S(1)}, f32[24,1280]{1,0:T(8,128)S(1)}, u32[]{:S(2)}, u32[]{:S(2)}) collective-permute-start(f32[24,1280]{1,0:T(8,128)S(1)} %select_add_fusion.1), channel_id=1, source_target_pairs={{0,192},{16,208},{32,224},{48,240},{64,256},{80,272},{96,288},{112... | collective-permute-start | bytes 368648 | tf_op jit(solution)/shard_map/ppermute | solution.py:36
  131.6 8.5 %collective-permute-start.8 = (f32[24,2560]{1,0:T(8,128)S(1)}, f32[24,2560]{1,0:T(8,128)S(1)}, u32[]{:S(2)}, u32[]{:S(2)}) collective-permute-start(f32[24,2560]{1,0:T(8,128)S(1)} %pad_maximum_fusion.1), channel_id=1, source_target_pairs={{0,384},{16,400},{32,416},{48,432},{64,448},{80,464},{96,480},{112... | collective-permute-start | bytes 737288 | tf_op jit(solution)/shard_map/ppermute | solution.py:36
  140.1 7.2 %copy-start.1 = (bf16[48,5120]{1,0:T(8,128)(2,1)S(1)}, bf16[48,5120]{1,0:T(8,128)(2,1)}, u32[]{:S(2)}) copy-start(bf16[48,5120]{1,0:T(8,128)(2,1)} %param.8) | copy-start | bytes 1474564
  140.2 7.2 %copy-start.2 = (f32[48,5120]{1,0:T(8,128)S(1)}, f32[48,5120]{1,0:T(8,128)}, u32[]{:S(2)}) copy-start(f32[48,5120]{1,0:T(8,128)} %param.11) | copy-start | bytes 2949124
  140.2 7.0 %collective-permute-start.9 = (f32[24,5120]{1,0:T(8,128)S(1)}, f32[24,5120]{1,0:T(8,128)S(1)}, u32[]{:S(2)}, u32[]{:S(2)}) collective-permute-start(f32[24,5120]{1,0:T(8,128)S(1)} %pad_maximum_fusion), channel_id=1, source_target_pairs={{0,16},{16,0},{32,48},{48,32},{64,80},{80,64},{96,112},{112,96},{1... | collective-permute-start | bytes 1474568 | tf_op jit(solution)/shard_map/ppermute | solution.py:36
Sparse Core Ops, SparseCore 0:
  10.4 89.5 all-gather.5
  102.3 81.0 all-gather.3

commit v3 on v2

--- a/solution.py
+++ b/solution.py
@@ -6,6 +6,7 @@
 from jax.sharding import PartitionSpec as P
 
 Y, ZH, ZL, X, C = 8, 2, 6, 4, 2
+RING = 48
 
 
 def moved(to):
@@ -36,23 +37,28 @@
     return lax.ppermute(array, ("rep", "fsdp"), pairs)
 
 
-def product(slot, tokens, weights, total, out_dtype):
-    rows, depth = tokens.shape[1:]
-    width = weights.shape[1]
+def product(slot, pairs, total, out_dtype):
+    rows, width = pairs[0][0].shape[1], pairs[0][1].shape[1]
     tile = width // 2
 
     def kernel(slot_ref, *refs):
         del slot_ref
-        acc = jnp.dot(refs[0][0], refs[1][...], preferred_element_type=jnp.float32)
-        if total is not None:
-            acc += refs[2][...]
+        acc = None if total is None else refs[-2][...]
+        for i in range(len(pairs)):
+            left, right = refs[2 * i][0], refs[2 * i + 1][...]
+            term = jnp.dot(left, right, preferred_element_type=jnp.float32)
+            acc = term if acc is None else acc + term
         refs[-1][...] = acc.astype(out_dtype)
 
-    in_specs = [
-        pl.BlockSpec((1, rows, depth), lambda j, at: (at[0], 0, 0)),
-        pl.BlockSpec((depth, tile), lambda j, at: (0, j)),
-    ]
-    operands = [slot, tokens, weights]
+    in_specs, operands, depth = [], [slot], 0
+    for tokens, weights in pairs:
+        if tokens.shape[0] == ZH:
+            in_specs.append(pl.BlockSpec((1,) + tokens.shape[1:], lambda j, at: (at[0], 0, 0)))
+        else:
+            in_specs.append(pl.BlockSpec((1,) + tokens.shape[1:], lambda j, at: (0, 0, 0)))
+        in_specs.append(pl.BlockSpec((weights.shape[0], tile), lambda j, at: (0, j)))
+        operands += [tokens, weights]
+        depth += weights.shape[0]
     if total is not None:
         in_specs.append(pl.BlockSpec((rows, tile), lambda j, at: (0, j)))
         operands.append(total)
@@ -74,12 +80,25 @@
     )(*operands)
 
 
-def fragment_term(base_wide, local_frag, block_exps):
-    exps = block_exps.astype(jnp.float32)
-    scale = jnp.repeat(jnp.exp2(exps), 128, axis=1)
-    inverse = jnp.repeat(jnp.exp2(-exps), 128, axis=1)
-    level = jnp.clip((base_wide - local_frag.astype(jnp.float32)) * inverse, -1.0, 1.0)
-    return level.astype(jnp.bfloat16) * scale.astype(jnp.bfloat16)
+def fragment_term(base_frag, local_frag, block_exps):
+    def kernel(base, local, exps, out):
+        power = exps[...].astype(jnp.float32)
+        scale = jnp.exp2(power).astype(jnp.bfloat16).astype(jnp.float32)
+        inverse = jnp.exp2(-power).astype(jnp.bfloat16).astype(jnp.float32)
+        for block in range(exps.shape[1]):
+            at = pl.ds(block * 128, 128)
+            gap = base[:, at].astype(jnp.float32) - local[:, at].astype(jnp.float32)
+            level = jnp.clip(gap * inverse[:, block : block + 1], -1.0, 1.0)
+            level = level.astype(jnp.bfloat16).astype(jnp.float32)
+            out[:, at] = (level * scale[:, block : block + 1]).astype(jnp.bfloat16)
+
+    return pl.pallas_call(
+        kernel,
+        in_specs=[pl.BlockSpec(memory_space=pltpu.VMEM)] * 3,
+        out_specs=pl.BlockSpec(memory_space=pltpu.VMEM),
+        out_shape=jax.ShapeDtypeStruct(base_frag.shape, jnp.bfloat16),
+        cost_estimate=pl.CostEstimate(flops=0, bytes_accessed=4 << 20, transcendentals=0),
+    )(base_frag, local_frag, block_exps)
 
 
 def keep_and_send(array, index, axis):
@@ -106,29 +125,45 @@
 
 def per_device(attn_heads, proj_weight, base_frag, local_frag, block_exps, momentum):
     own = proj_weight[0]
-    h = lax.axis_index("fsdp") % ZH
+    index = lax.axis_index("fsdp")
+    y, h = index // ZH, index % ZH
     index = lax.axis_index("rep")
     core, z, x = index % C, (index // C) % ZL, index // (C * ZL)
     far, near, third = x // 2, x % 2, z // 2
     base_wide = base_frag.astype(jnp.float32)
 
-    gathered = gather_y(own)
+    depth = own.shape[0]
+    whole = depth - RING
+    gathered = gather_y(own[:whole])
     other = send_to(own, CROSS)
-    keep, give = keep_and_send(fragment_term(base_wide, local_frag[0], block_exps[0]), core, 0)
+    term = fragment_term(base_frag, local_frag[0], block_exps[0])
+    term, mine = together(term, own[whole:])
+    up1, down1 = send_to(mine, UP), send_to(mine, DOWN)
+    up2, down2 = send_to(up1, UP), send_to(down1, DOWN)
+    keep, give = keep_and_send(term, core, 0)
     part = keep.astype(jnp.float32) + send_to(give, CORE).astype(jnp.float32)
     keep, give = keep_and_send(part, far, 1)
     part = keep + send_to(give, X_FAR)
     rows, width = attn_heads.shape
-    tokens = attn_heads.reshape(rows, Y, ZH, width // (Y * ZH)).transpose(2, 0, 1, 3)
-    tokens = tokens.reshape(ZH, rows, width // ZH)
-    other, part, tokens = together(other, part, tokens)
+    shards = attn_heads.reshape(rows, Y, ZH, depth).transpose(2, 0, 1, 3)
+    tokens = shards.reshape(ZH, rows, width // ZH)
+    near_tokens = shards[..., :whole].reshape(ZH, rows, Y * whole)
+    turned = jnp.where(h == 0, shards[0], shards[1])[..., whole:]
+    turned = lax.dynamic_slice_in_dim(jnp.concatenate([turned, turned], axis=1), y, Y, 1)
+    turned = turned.reshape(1, rows, Y * RING)
+    other, part, tokens, near_tokens, turned, up2, down2 = together(
+        other, part, tokens, near_tokens, turned, up2, down2
+    )
 
     over_gathered = gather_y(other)
+    up3, down3 = send_to(up2, UP), send_to(down2, DOWN)
+    up4 = send_to(up3, UP)
+    ringed = jnp.concatenate([mine, down1, down2, down3, up4, up3, up2, up1], axis=0)
     keep, give = keep_and_send(part, near, 1)
     part = keep + send_to(give, X_NEAR)
-    total = product(h[None].astype(jnp.int32), tokens, gathered, None, jnp.float32)
+    pairs = [(near_tokens, gathered), (turned, ringed)]
+    total = product(h[None].astype(jnp.int32), pairs, None, jnp.float32)
     part = part + send_to(part, Z_PAIR)
-    part, total = together(part, total)
     two, four = send_to(part, Z_TWO), send_to(part, Z_FOUR)
     zero = jnp.where(third == 0, part, jnp.where(third == 1, two, four))
     one = jnp.where(third == 1, part, jnp.where(third == 2, two, four))
@@ -141,7 +176,8 @@
     new_base = (base_wide - 0.7 * (outer_grad + 0.9 * new_momentum)).astype(jnp.bfloat16)
 
     total, new_momentum, new_base = together(total, new_momentum, new_base)
-    mixed = product((1 - h)[None].astype(jnp.int32), tokens, over_gathered, total, jnp.bfloat16)
+    pairs = [(tokens, over_gathered)]
+    mixed = product((1 - h)[None].astype(jnp.int32), pairs, total, jnp.bfloat16)
     return mixed, new_base, new_momentum
 
 

time: 196 us -> 201 us (1.026)
  waiting for transfers between devices: 80.9 us -> 57.2 us
  local copies, waits for them, and re-layouts: 4.03 us -> 20.4 us
  starting transfers between devices: 81.8 us -> 86.2 us
  other arithmetic: 3.84 us -> 7.87 us
  Pallas kernels: 10.9 us -> 13.7 us
    ppermute x10 -> x17, waiting for transfers between devices: 45.2 us -> 30.2 us  [send_to(): return lax.ppermute(array, ('rep', 'fsdp'), pairs)]
    unnamed x9 -> x19, local copies, waits for them, and re-layouts: 1.67 us -> 9.95 us
    all_gather x2, waiting for transfers between devices: 35.1 us -> 27 us  [gather_y(): lax.all_gather(array, 'fsdp', axis=0, tiled=True, axis_index_groups=groups)]
    slice x0 -> x6, local copies, waits for them, and re-layouts: none -> 5.18 us  [the longest x2 2.25 us: per_device(): near_tokens = shards[..., :whole].reshape(ZH, rows, Y * whole)]
    ppermute x10 -> x17, starting transfers between devices: 81.7 us -> 86.1 us  [send_to(): return lax.ppermute(array, ('rep', 'fsdp'), pairs)]
    select_n x3, other arithmetic: 0.07 us -> 2.52 us  [keep_and_send(): jnp.where(index == 0, second, first)]
    pallas_call x0 -> x1, Pallas kernels: none -> 2.36 us  [fragment_term(): pl.pallas_call(kernel, in_specs=[pl.BlockSpec(memory_space=pltpu.VMEM)] *...]
    optimization_barrier x1 -> x3, local copies, waits for them, and re-layouts: 1.47 us -> 3.52 us  [together(): return lax.optimization_barrier(arrays)]
  transfers between devices with their start and end apart: 12 -> 19, of which waited for: 10 -> 8; matrix products, arithmetic and copies ran while one was open for 4% -> 13% of each run, Pallas kernels for 3% -> 4%
where the time goes in v3:
time: 201 us; the launch traced here: 200 us
  starting transfers between devices  86.2 us (43%)
  waiting for transfers between devices  57.2 us (28%)
  local copies, waits for them, and re-layouts  20.4 us (10%)
  between operations  14.5 us (7%)
  Pallas kernels  13.7 us (7%)
  other arithmetic  7.87 us (4%)
    ppermute x17, starting transfers between devices, send_to(): return lax.ppermute(array, ('rep', 'fsdp'), pairs)  86.1 us
    ppermute x17, waiting for transfers between devices, send_to(): return lax.ppermute(array, ('rep', 'fsdp'), pairs)  30.2 us
    all_gather x2, waiting for transfers between devices, gather_y(): lax.all_gather(array, 'fsdp', axis=0, tiled=True, axis_index_groups=groups)  27 us
    pallas_call x2, Pallas kernels, product(): pl.pallas_call(kernel, grid_spec=pltpu.PrefetchScalarGridSpec(num_scalar_...  11.3 us
    unnamed x19, local copies, waits for them, and re-layouts  9.95 us
  transfers between devices with their start and end apart: 19, of which 8 were waited for; matrix products, arithmetic and copies ran while one was open for 13% of the time, Pallas kernels for 4%

profile of v3, /device:TPU:1, one launch (start us, length us, event | category | flops | bytes accessed | tf_op | source)
XLA Modules:
  0.0 199.8 jit_solution(2723683513712104057)
XLA Ops:
  7.2 1.9 slice.52
  10.7 2.4 %shard_map.85 = bf16[48,5120]{1,0:T(8,128)(2,1)} custom-call(bf16[48,5120]{1,0:T(8,128)(2,1)} %base.1, bf16[48,5120]{1,0:T(8,128)(2,1)} %bitcast.23, s32[48,40]{1,0:T(8,128)} %bitcast.24), custom_call_target="tpu_custom_call" | custom-call | bytes 4194304 | tf_op jit(solution)/shard_map/pallas_call | solution.py:95
  14.1 1.8 broadcast_select_fusion.2
  15.9 12.4 %collective-permute-start.1 = (bf16[24,5120]{1,0:T(8,128)(2,1)}, bf16[24,5120]{1,0:T(8,128)(2,1)}, u32[]{:S(2)}, u32[]{:S(2)}) collective-permute-start(bf16[24,5120]{1,0:T(8,128)(2,1)} %broadcast_select_fusion.2), channel_id=1, source_target_pairs={{0,16},{16,0},{32,48},{48,32},{64,80},{80,64},{96,112},{112,96},{1... | collective-permute-start | bytes 737288 | tf_op jit(solution)/shard_map/ppermute | solution.py:37
  28.3 1.9 collective-permute-start.3
  30.2 4.6 %collective-permute-start.5 = (bf16[48,2560]{1,0:T(8,128)(2,1)S(1)}, bf16[48,2560]{1,0:T(8,128)(2,1)}, u32[]{:S(2)}, u32[]{:S(2)}) collective-permute-start(bf16[48,2560]{1,0:T(8,128)(2,1)S(1)} %slice_bitcast_fusion), channel_id=1, source_target_pairs={{0,14},{16,30},{32,46},{48,62},{64,78},{80,94},{96,110},{112,126},... | collective-permute-start | bytes 737288 | tf_op jit(solution)/shard_map/ppermute | solution.py:37
  34.8 6.4 %collective-permute-start = (bf16[160,2560]{1,0:T(8,128)(2,1)}, bf16[160,2560]{1,0:T(8,128)(2,1)}, u32[]{:S(2)}, u32[]{:S(2)}) collective-permute-start(bf16[160,2560]{1,0:T(8,128)(2,1)} %bitcast.1), channel_id=1, source_target_pairs={{0,1},{16,17},{32,33},{48,49},{64,65},{80,81},{96,97},{112,113},{1... | collective-permute-start | bytes 2457608 | tf_op jit(solution)/shard_map/ppermute | solution.py:37
  43.7 4.6 %collective-permute-start.2 = (f32[24,2560]{1,0:T(8,128)}, f32[24,2560]{1,0:T(8,128)}, u32[]{:S(2)}, u32[]{:S(2)}) collective-permute-start(f32[24,2560]{1,0:T(8,128)} %slice_select_fusion.1), channel_id=1, source_target_pairs={{0,384},{16,400},{32,416},{48,432},{64,448},{80,464},{96,480},{112... | collective-permute-start | bytes 737288 | tf_op jit(solution)/shard_map/ppermute | solution.py:37
  52.4 1.9 collective-permute-start.4
  54.3 4.6 %collective-permute-start.6 = (bf16[48,2560]{1,0:T(8,128)(2,1)}, bf16[48,2560]{1,0:T(8,128)(2,1)}, u32[]{:S(2)}, u32[]{:S(2)}) collective-permute-start(bf16[48,2560]{1,0:T(8,128)(2,1)} %collective-permute-done.5), channel_id=1, source_target_pairs={{0,14},{16,30},{32,46},{48,62},{64,78},{80,94},{96,110},{112,126},... | collective-permute-start | bytes 737288 | tf_op jit(solution)/shard_map/ppermute | solution.py:37
  59.9 8.4 %collective-permute-done.4 = bf16[48,2560]{1,0:T(8,128)(2,1)} collective-permute-done((bf16[48,2560]{1,0:T(8,128)(2,1)}, bf16[48,2560]{1,0:T(8,128)(2,1)}, u32[]{:S(2)}, u32[]{:S(2)}) %collective-permute-start.4) | collective-permute-done | bytes 245792 | tf_op jit(solution)/shard_map/ppermute | solution.py:37
  69.7 9.2 %collective-permute-done = bf16[160,2560]{1,0:T(8,128)(2,1)} collective-permute-done((bf16[160,2560]{1,0:T(8,128)(2,1)}, bf16[160,2560]{1,0:T(8,128)(2,1)}, u32[]{:S(2)}, u32[]{:S(2)}) %collective-permute-start) | collective-permute-done | bytes 819232 | tf_op jit(solution)/shard_map/ppermute | solution.py:37
  78.9 1.9 collective-permute-start.10
  81.6 3.4 %collective-permute-done.10 = f32[24,1280]{1,0:T(8,128)S(1)} collective-permute-done((f32[24,1280]{1,0:T(8,128)S(1)}, f32[24,1280]{1,0:T(8,128)S(1)}, u32[]{:S(2)}, u32[]{:S(2)}) %collective-permute-start.10) | collective-permute-done | bytes 122912 | tf_op jit(solution)/shard_map/ppermute | solution.py:37
  85.0 19.1 %collective-permute-start.11 = (f32[24,1280]{1,0:T(8,128)S(1)}, f32[24,1280]{1,0:T(8,128)S(1)}, u32[]{:S(2)}, u32[]{:S(2)}) collective-permute-start(f32[24,1280]{1,0:T(8,128)S(1)} %select_add_fusion.2), channel_id=1, source_target_pairs={{0,32},{16,48},{32,0},{48,16},{64,96},{80,112},{96,64},{112,80},{1... | collective-permute-start | bytes 368648 | tf_op jit(solution)/shard_map/ppermute | solution.py:37
  105.7 3.0 %collective-permute-start.7 = (bf16[48,2560]{1,0:T(8,128)(2,1)}, bf16[48,2560]{1,0:T(8,128)(2,1)S(1)}, u32[]{:S(2)}, u32[]{:S(2)}) collective-permute-start(bf16[48,2560]{1,0:T(8,128)(2,1)} %collective-permute-done.6), channel_id=1, source_target_pairs={{0,14},{16,30},{32,46},{48,62},{64,78},{80,94},{96,110},{112,126},... | collective-permute-start | bytes 737288 | tf_op jit(solution)/shard_map/ppermute | solution.py:37
  108.7 2.2 %collective-permute-start.8 = (bf16[48,2560]{1,0:T(8,128)(2,1)}, bf16[48,2560]{1,0:T(8,128)(2,1)S(1)}, u32[]{:S(2)}, u32[]{:S(2)}) collective-permute-start(bf16[48,2560]{1,0:T(8,128)(2,1)} %collective-permute-done.4), channel_id=1, source_target_pairs={{0,2},{16,18},{32,34},{48,50},{64,66},{80,82},{96,98},{112,114},{1... | collective-permute-start | bytes 737288 | tf_op jit(solution)/shard_map/ppermute | solution.py:37
  111.0 1.9 collective-permute-start.12
  113.0 7.3 %collective-permute-start.13 = (f32[24,1280]{1,0:T(8,128)S(1)}, f32[24,1280]{1,0:T(8,128)S(1)}, u32[]{:S(2)}, u32[]{:S(2)}) collective-permute-start(f32[24,1280]{1,0:T(8,128)S(1)} %add.53), channel_id=1, source_target_pairs={{0,128},{16,144},{32,160},{48,176},{64,0},{80,16},{96,32},{112,48}... | collective-permute-start | bytes 368648 | tf_op jit(solution)/shard_map/ppermute | solution.py:37
  120.2 1.7 constant_dynamic-update-slice_fusion.5
  125.4 1.9 collective-permute-start.9
  127.4 2.5 %collective-permute-done.13 = f32[24,1280]{1,0:T(8,128)S(1)} collective-permute-done((f32[24,1280]{1,0:T(8,128)S(1)}, f32[24,1280]{1,0:T(8,128)S(1)}, u32[]{:S(2)}, u32[]{:S(2)}) %collective-permute-start.13) | collective-permute-done | bytes 122912 | tf_op jit(solution)/shard_map/ppermute | solution.py:37
  129.9 3.1 %collective-permute-start.14 = (f32[24,1280]{1,0:T(8,128)S(1)}, f32[24,1280]{1,0:T(8,128)S(1)}, u32[]{:S(2)}, u32[]{:S(2)}) collective-permute-start(f32[24,1280]{1,0:T(8,128)S(1)} %select_add_fusion.1), channel_id=1, source_target_pairs={{0,192},{16,208},{32,224},{48,240},{64,256},{80,272},{96,288},{112... | collective-permute-start | bytes 368648 | tf_op jit(solution)/shard_map/ppermute | solution.py:37
  133.7 2.2 %collective-permute-done.14 = f32[24,1280]{1,0:T(8,128)S(1)} collective-permute-done((f32[24,1280]{1,0:T(8,128)S(1)}, f32[24,1280]{1,0:T(8,128)S(1)}, u32[]{:S(2)}, u32[]{:S(2)}) %collective-permute-start.14) | collective-permute-done | bytes 122912 | tf_op jit(solution)/shard_map/ppermute | solution.py:37
  136.0 4.6 %collective-permute-start.15 = (f32[24,2560]{1,0:T(8,128)S(1)}, f32[24,2560]{1,0:T(8,128)S(1)}, u32[]{:S(2)}, u32[]{:S(2)}) collective-permute-start(f32[24,2560]{1,0:T(8,128)S(1)} %pad_maximum_fusion.1), channel_id=1, source_target_pairs={{0,384},{16,400},{32,416},{48,432},{64,448},{80,464},{96,480},{112... | collective-permute-start | bytes 737288 | tf_op jit(solution)/shard_map/ppermute | solution.py:37
  142.0 3.1 %collective-permute-done.15 = f32[24,2560]{1,0:T(8,128)S(1)} collective-permute-done((f32[24,2560]{1,0:T(8,128)S(1)}, f32[24,2560]{1,0:T(8,128)S(1)}, u32[]{:S(2)}, u32[]{:S(2)}) %collective-permute-start.15) | collective-permute-done | bytes 245792 | tf_op jit(solution)/shard_map/ppermute | solution.py:37
  145.2 4.7 %collective-permute-start.16 = (f32[24,5120]{1,0:T(8,128)S(1)}, f32[24,5120]{1,0:T(8,128)S(1)}, u32[]{:S(2)}, u32[]{:S(2)}) collective-permute-start(f32[24,5120]{1,0:T(8,128)S(1)} %pad_maximum_fusion), channel_id=1, source_target_pairs={{0,16},{16,0},{32,48},{48,32},{64,80},{80,64},{96,112},{112,96},{1... | collective-permute-start | bytes 1474568 | tf_op jit(solution)/shard_map/ppermute | solution.py:37
  149.9 1.7 constant_dynamic-update-slice_fusion.1
  151.6 1.7 constant_dynamic-update-slice_fusion.refs_3_
  154.7 5.6 %shard_map.86.refs_2_ = f32[256,2560]{1,0:T(8,128)} custom-call(s32[1]{0:T(128)} %bitcast.12.slot_ref, bf16[2,256,896]{2,1,0:T(8,128)(2,1)} %copy.15.refs_0_, bf16[896,2560]{1,0:T(8,128)(2,1)} %bitcast.20, bf16[1,256,384]{2,1,0:T(8,128)(2,1)} %copy.16.refs_2_, bf16[384,2560]{1,0:T(8,128)(2,1)} %constant_dynamic-update-slice_fusion.refs_3_), custom_call_target="tpu_custom_call" | custom-call | flops 1677721600 | bytes 10485760 | tf_op jit(solution)/shard_map/pallas_call | solution.py:65
  160.4 27.0 %all-gather.4.cloned.1.call-done.refs_1_ = bf16[1280,2560]{1,0:T(8,128)(2,1)} async-done(((bf16[160,2560]{1,0:T(8,128)(2,1)}), bf16[1280,2560]{1,0:T(8,128)(2,1)}) %all-gather.4.cloned.1.call-update) | async-done | bytes 6553616 | tf_op jit(solution)/shard_map/all_gather | solution.py:123
  187.3 5.7 %shard_map.87 = bf16[256,2560]{1,0:T(8,128)(2,1)} custom-call(s32[1]{0:T(128)} %bitcast.slot_ref, bf16[2,256,1280]{2,1,0:T(8,128)(2,1)} %copy.17.refs_0_, bf16[1280,2560]{1,0:T(8,128)(2,1)} %all-gather.4.cloned.1.call-done.refs_1_, f32[256,2560]{1,0:T(8,128)} %shard_map.86.refs_2_), custom_call_target="tpu_custom_call" | custom-call | flops 1677721600 | bytes 10485760 | tf_op jit(solution)/shard_map/pallas_call | solution.py:65
  (57 shorter events, 21.1 us)
Async XLA Ops:
  7.2 147.6 %all-gather.6.cloned.1.call-start = ((), (), s32[]{:S(2)}) async-start(), calls=%async_computation.1 | async-start | bytes 5160960 | tf_op jit(solution)/shard_map/all_gather | solution.py:123
  9.1 32.1 %copy-start.2 = (bf16[256,2560]{1,0:T(8,128)(2,1)S(1)}, bf16[256,2560]{1,0:T(8,128)(2,1)}, u32[]{:S(2)}) copy-start(bf16[256,2560]{1,0:T(8,128)(2,1)} %param.6) | copy-start | bytes 3932164
  9.1 178.2 %all-gather.4.cloned.1.call-start = ((), (), s32[]{:S(2)}) async-start(), calls=%async_computation | async-start | bytes 7372800 | tf_op jit(solution)/shard_map/all_gather | solution.py:123
  13.1 28.8 %copy-start = (bf16[48,5120]{1,0:T(8,128)(2,1)S(1)}, bf16[48,5120]{1,0:T(8,128)(2,1)}, u32[]{:S(2)}) copy-start(bf16[48,5120]{1,0:T(8,128)(2,1)} %shard_map.85) | copy-start | bytes 1474564
  15.9 26.0 %collective-permute-start.1 = (bf16[24,5120]{1,0:T(8,128)(2,1)}, bf16[24,5120]{1,0:T(8,128)(2,1)}, u32[]{:S(2)}, u32[]{:S(2)}) collective-permute-start(bf16[24,5120]{1,0:T(8,128)(2,1)} %broadcast_select_fusion.2), channel_id=1, source_target_pairs={{0,16},{16,0},{32,48},{48,32},{64,80},{80,64},{96,112},{112,96},{1... | collective-permute-start | bytes 737288 | tf_op jit(solution)/shard_map/ppermute | solution.py:37
  28.3 24.1 %collective-permute-start.3 = (bf16[48,2560]{1,0:T(8,128)(2,1)S(1)}, bf16[48,2560]{1,0:T(8,128)(2,1)}, u32[]{:S(2)}, u32[]{:S(2)}) collective-permute-start(bf16[48,2560]{1,0:T(8,128)(2,1)S(1)} %slice_bitcast_fusion), channel_id=1, source_target_pairs={{0,2},{16,18},{32,34},{48,50},{64,66},{80,82},{96,98},{112,114},{1... | collective-permute-start | bytes 737288 | tf_op jit(solution)/shard_map/ppermute | solution.py:37
  30.2 24.1 %collective-permute-start.5 = (bf16[48,2560]{1,0:T(8,128)(2,1)S(1)}, bf16[48,2560]{1,0:T(8,128)(2,1)}, u32[]{:S(2)}, u32[]{:S(2)}) collective-permute-start(bf16[48,2560]{1,0:T(8,128)(2,1)S(1)} %slice_bitcast_fusion), channel_id=1, source_target_pairs={{0,14},{16,30},{32,46},{48,62},{64,78},{80,94},{96,110},{112,126},... | collective-permute-start | bytes 737288 | tf_op jit(solution)/shard_map/ppermute | solution.py:37
  34.8 44.1 %collective-permute-start = (bf16[160,2560]{1,0:T(8,128)(2,1)}, bf16[160,2560]{1,0:T(8,128)(2,1)}, u32[]{:S(2)}, u32[]{:S(2)}) collective-permute-start(bf16[160,2560]{1,0:T(8,128)(2,1)} %bitcast.1), channel_id=1, source_target_pairs={{0,1},{16,17},{32,33},{48,49},{64,65},{80,81},{96,97},{112,113},{1... | collective-permute-start | bytes 2457608 | tf_op jit(solution)/shard_map/ppermute | solution.py:37
  43.7 15.2 %collective-permute-start.2 = (f32[24,2560]{1,0:T(8,128)}, f32[24,2560]{1,0:T(8,128)}, u32[]{:S(2)}, u32[]{:S(2)}) collective-permute-start(f32[24,2560]{1,0:T(8,128)} %slice_select_fusion.1), channel_id=1, source_target_pairs={{0,384},{16,400},{32,416},{48,432},{64,448},{80,464},{96,480},{112... | collective-permute-start | bytes 737288 | tf_op jit(solution)/shard_map/ppermute | solution.py:37
  50.2 1.4 slice-start
  52.4 15.9 %collective-permute-start.4 = (bf16[48,2560]{1,0:T(8,128)(2,1)}, bf16[48,2560]{1,0:T(8,128)(2,1)}, u32[]{:S(2)}, u32[]{:S(2)}) collective-permute-start(bf16[48,2560]{1,0:T(8,128)(2,1)} %collective-permute-done.3), channel_id=1, source_target_pairs={{0,2},{16,18},{32,34},{48,50},{64,66},{80,82},{96,98},{112,114},{1... | collective-permute-start | bytes 737288 | tf_op jit(solution)/shard_map/ppermute | solution.py:37
  54.3 15.4 %collective-permute-start.6 = (bf16[48,2560]{1,0:T(8,128)(2,1)}, bf16[48,2560]{1,0:T(8,128)(2,1)}, u32[]{:S(2)}, u32[]{:S(2)}) collective-permute-start(bf16[48,2560]{1,0:T(8,128)(2,1)} %collective-permute-done.5), channel_id=1, source_target_pairs={{0,14},{16,30},{32,46},{48,62},{64,78},{80,94},{96,110},{112,126},... | collective-permute-start | bytes 737288 | tf_op jit(solution)/shard_map/ppermute | solution.py:37
  78.9 6.0 %collective-permute-start.10 = (f32[24,1280]{1,0:T(8,128)S(1)}, f32[24,1280]{1,0:T(8,128)S(1)}, u32[]{:S(2)}, u32[]{:S(2)}) collective-permute-start(f32[24,1280]{1,0:T(8,128)S(1)} %slice_select_fusion.2), channel_id=1, source_target_pairs={{0,192},{16,208},{32,224},{48,240},{64,256},{80,272},{96,288},{112... | collective-permute-start | bytes 368648 | tf_op jit(solution)/shard_map/ppermute | solution.py:37
  81.6 41.6 %copy-start.4 = (bf16[256,8,48]{0,2,1:T(8,128)(2,1)S(1)}, bf16[256,8,48]{0,2,1:T(8,128)(2,1)}, u32[]{:S(2)}) copy-start(bf16[256,8,48]{0,2,1:T(8,128)(2,1)} %fusion.1) | copy-start | bytes 589828
  85.0 26.0 %collective-permute-start.11 = (f32[24,1280]{1,0:T(8,128)S(1)}, f32[24,1280]{1,0:T(8,128)S(1)}, u32[]{:S(2)}, u32[]{:S(2)}) collective-permute-start(f32[24,1280]{1,0:T(8,128)S(1)} %select_add_fusion.2), channel_id=1, source_target_pairs={{0,32},{16,48},{32,0},{48,16},{64,96},{80,112},{96,64},{112,80},{1... | collective-permute-start | bytes 368648 | tf_op jit(solution)/shard_map/ppermute | solution.py:37
  105.7 27.3 %collective-permute-start.7 = (bf16[48,2560]{1,0:T(8,128)(2,1)}, bf16[48,2560]{1,0:T(8,128)(2,1)S(1)}, u32[]{:S(2)}, u32[]{:S(2)}) collective-permute-start(bf16[48,2560]{1,0:T(8,128)(2,1)} %collective-permute-done.6), channel_id=1, source_target_pairs={{0,14},{16,30},{32,46},{48,62},{64,78},{80,94},{96,110},{112,126},... | collective-permute-start | bytes 737288 | tf_op jit(solution)/shard_map/ppermute | solution.py:37
  108.7 16.7 %collective-permute-start.8 = (bf16[48,2560]{1,0:T(8,128)(2,1)}, bf16[48,2560]{1,0:T(8,128)(2,1)S(1)}, u32[]{:S(2)}, u32[]{:S(2)}) collective-permute-start(bf16[48,2560]{1,0:T(8,128)(2,1)} %collective-permute-done.4), channel_id=1, source_target_pairs={{0,2},{16,18},{32,34},{48,50},{64,66},{80,82},{96,98},{112,114},{1... | collective-permute-start | bytes 737288 | tf_op jit(solution)/shard_map/ppermute | solution.py:37
  111.0 16.3 %collective-permute-start.12 = (f32[24,1280]{1,0:T(8,128)S(1)}, f32[24,1280]{1,0:T(8,128)S(1)}, u32[]{:S(2)}, u32[]{:S(2)}) collective-permute-start(f32[24,1280]{1,0:T(8,128)S(1)} %add.53), channel_id=1, source_target_pairs={{0,64},{16,80},{32,96},{48,112},{64,128},{80,144},{96,160},{112,17... | collective-permute-start | bytes 368648 | tf_op jit(solution)/shard_map/ppermute | solution.py:37
  113.0 16.9 %collective-permute-start.13 = (f32[24,1280]{1,0:T(8,128)S(1)}, f32[24,1280]{1,0:T(8,128)S(1)}, u32[]{:S(2)}, u32[]{:S(2)}) collective-permute-start(f32[24,1280]{1,0:T(8,128)S(1)} %add.53), channel_id=1, source_target_pairs={{0,128},{16,144},{32,160},{48,176},{64,0},{80,16},{96,32},{112,48}... | collective-permute-start | bytes 368648 | tf_op jit(solution)/shard_map/ppermute | solution.py:37
  125.4 15.2 %collective-permute-start.9 = (bf16[48,2560]{1,0:T(8,128)(2,1)S(1)}, bf16[48,2560]{1,0:T(8,128)(2,1)S(1)}, u32[]{:S(2)}, u32[]{:S(2)}) collective-permute-start(bf16[48,2560]{1,0:T(8,128)(2,1)S(1)} %collective-permute-done.8), channel_id=1, source_target_pairs={{0,2},{16,18},{32,34},{48,50},{64,66},{80,82},{96,98},{112,114},{1... | collective-permute-start | bytes 737288 | tf_op jit(solution)/shard_map/ppermute | solution.py:37
  129.9 6.0 %collective-permute-start.14 = (f32[24,1280]{1,0:T(8,128)S(1)}, f32[24,1280]{1,0:T(8,128)S(1)}, u32[]{:S(2)}, u32[]{:S(2)}) collective-permute-start(f32[24,1280]{1,0:T(8,128)S(1)} %select_add_fusion.1), channel_id=1, source_target_pairs={{0,192},{16,208},{32,224},{48,240},{64,256},{80,272},{96,288},{112... | collective-permute-start | bytes 368648 | tf_op jit(solution)/shard_map/ppermute | solution.py:37
  136.0 9.1 %collective-permute-start.15 = (f32[24,2560]{1,0:T(8,128)S(1)}, f32[24,2560]{1,0:T(8,128)S(1)}, u32[]{:S(2)}, u32[]{:S(2)}) collective-permute-start(f32[24,2560]{1,0:T(8,128)S(1)} %pad_maximum_fusion.1), channel_id=1, source_target_pairs={{0,384},{16,400},{32,416},{48,432},{64,448},{80,464},{96,480},{112... | collective-permute-start | bytes 737288 | tf_op jit(solution)/shard_map/ppermute | solution.py:37
  145.2 8.2 %copy-start.1 = (bf16[48,5120]{1,0:T(8,128)(2,1)S(1)}, bf16[48,5120]{1,0:T(8,128)(2,1)}, u32[]{:S(2)}) copy-start(bf16[48,5120]{1,0:T(8,128)(2,1)} %base.1) | copy-start | bytes 1474564
  145.2 8.2 %copy-start.3 = (f32[48,5120]{1,0:T(8,128)S(1)}, f32[48,5120]{1,0:T(8,128)}, u32[]{:S(2)}) copy-start(f32[48,5120]{1,0:T(8,128)} %param.11) | copy-start | bytes 2949124
  145.2 8.0 %collective-permute-start.16 = (f32[24,5120]{1,0:T(8,128)S(1)}, f32[24,5120]{1,0:T(8,128)S(1)}, u32[]{:S(2)}, u32[]{:S(2)}) collective-permute-start(f32[24,5120]{1,0:T(8,128)S(1)} %pad_maximum_fusion), channel_id=1, source_target_pairs={{0,16},{16,0},{32,48},{48,32},{64,80},{80,64},{96,112},{112,96},{1... | collective-permute-start | bytes 1474568 | tf_op jit(solution)/shard_map/ppermute | solution.py:37
Sparse Core Ops, SparseCore 0:
  10.4 78.5 all-gather.5
  91.3 95.9 all-gather.3

commit v4 on v3

--- a/solution.py
+++ b/solution.py
@@ -80,25 +80,12 @@
     )(*operands)
 
 
-def fragment_term(base_frag, local_frag, block_exps):
-    def kernel(base, local, exps, out):
-        power = exps[...].astype(jnp.float32)
-        scale = jnp.exp2(power).astype(jnp.bfloat16).astype(jnp.float32)
-        inverse = jnp.exp2(-power).astype(jnp.bfloat16).astype(jnp.float32)
-        for block in range(exps.shape[1]):
-            at = pl.ds(block * 128, 128)
-            gap = base[:, at].astype(jnp.float32) - local[:, at].astype(jnp.float32)
-            level = jnp.clip(gap * inverse[:, block : block + 1], -1.0, 1.0)
-            level = level.astype(jnp.bfloat16).astype(jnp.float32)
-            out[:, at] = (level * scale[:, block : block + 1]).astype(jnp.bfloat16)
-
-    return pl.pallas_call(
-        kernel,
-        in_specs=[pl.BlockSpec(memory_space=pltpu.VMEM)] * 3,
-        out_specs=pl.BlockSpec(memory_space=pltpu.VMEM),
-        out_shape=jax.ShapeDtypeStruct(base_frag.shape, jnp.bfloat16),
-        cost_estimate=pl.CostEstimate(flops=0, bytes_accessed=4 << 20, transcendentals=0),
-    )(base_frag, local_frag, block_exps)
+def fragment_term(base_wide, local_frag, block_exps):
+    exps = block_exps.astype(jnp.float32)
+    scale = jnp.repeat(jnp.exp2(exps), 128, axis=1)
+    inverse = jnp.repeat(jnp.exp2(-exps), 128, axis=1)
+    level = jnp.clip((base_wide - local_frag.astype(jnp.float32)) * inverse, -1.0, 1.0)
+    return level.astype(jnp.bfloat16) * scale.astype(jnp.bfloat16)
 
 
 def keep_and_send(array, index, axis):
@@ -132,38 +119,35 @@
     far, near, third = x // 2, x % 2, z // 2
     base_wide = base_frag.astype(jnp.float32)
 
-    depth = own.shape[0]
-    whole = depth - RING
-    gathered = gather_y(own[:whole])
+    gathered = gather_y(own)
     other = send_to(own, CROSS)
-    term = fragment_term(base_frag, local_frag[0], block_exps[0])
-    term, mine = together(term, own[whole:])
-    up1, down1 = send_to(mine, UP), send_to(mine, DOWN)
-    up2, down2 = send_to(up1, UP), send_to(down1, DOWN)
-    keep, give = keep_and_send(term, core, 0)
+    keep, give = keep_and_send(fragment_term(base_wide, local_frag[0], block_exps[0]), core, 0)
     part = keep.astype(jnp.float32) + send_to(give, CORE).astype(jnp.float32)
     keep, give = keep_and_send(part, far, 1)
     part = keep + send_to(give, X_FAR)
     rows, width = attn_heads.shape
+    depth = own.shape[0]
+    whole = depth - RING
     shards = attn_heads.reshape(rows, Y, ZH, depth).transpose(2, 0, 1, 3)
     tokens = shards.reshape(ZH, rows, width // ZH)
-    near_tokens = shards[..., :whole].reshape(ZH, rows, Y * whole)
-    turned = jnp.where(h == 0, shards[0], shards[1])[..., whole:]
+    over_tokens = shards[..., :whole].reshape(ZH, rows, Y * whole)
+    turned = jnp.where(h == 0, shards[1], shards[0])[..., whole:]
     turned = lax.dynamic_slice_in_dim(jnp.concatenate([turned, turned], axis=1), y, Y, 1)
     turned = turned.reshape(1, rows, Y * RING)
-    other, part, tokens, near_tokens, turned, up2, down2 = together(
-        other, part, tokens, near_tokens, turned, up2, down2
-    )
+    other, part, tokens, over_tokens, turned = together(other, part, tokens, over_tokens, turned)
 
-    over_gathered = gather_y(other)
+    over_gathered = gather_y(other[:whole])
+    mine = other[whole:]
+    up1, down1 = send_to(mine, UP), send_to(mine, DOWN)
+    up2, down2 = send_to(up1, UP), send_to(down1, DOWN)
     up3, down3 = send_to(up2, UP), send_to(down2, DOWN)
     up4 = send_to(up3, UP)
     ringed = jnp.concatenate([mine, down1, down2, down3, up4, up3, up2, up1], axis=0)
     keep, give = keep_and_send(part, near, 1)
     part = keep + send_to(give, X_NEAR)
-    pairs = [(near_tokens, gathered), (turned, ringed)]
-    total = product(h[None].astype(jnp.int32), pairs, None, jnp.float32)
+    total = product(h[None].astype(jnp.int32), [(tokens, gathered)], None, jnp.float32)
     part = part + send_to(part, Z_PAIR)
+    part, total = together(part, total)
     two, four = send_to(part, Z_TWO), send_to(part, Z_FOUR)
     zero = jnp.where(third == 0, part, jnp.where(third == 1, two, four))
     one = jnp.where(third == 1, part, jnp.where(third == 2, two, four))
@@ -175,8 +159,8 @@
     new_momentum = 0.9 * momentum + outer_grad
     new_base = (base_wide - 0.7 * (outer_grad + 0.9 * new_momentum)).astype(jnp.bfloat16)
 
-    total, new_momentum, new_base = together(total, new_momentum, new_base)
-    pairs = [(tokens, over_gathered)]
+    total, ringed, new_momentum, new_base = together(total, ringed, new_momentum, new_base)
+    pairs = [(over_tokens, over_gathered), (turned, ringed)]
     mixed = product((1 - h)[None].astype(jnp.int32), pairs, total, jnp.bfloat16)
     return mixed, new_base, new_momentum
 

time: 201 us -> 195 us (0.970)
  local copies, waits for them, and re-layouts: 20.4 us -> 14 us
  starting transfers between devices: 86.2 us -> 89.4 us
  Pallas kernels: 13.7 us -> 11.3 us
    all_gather x2, waiting for transfers between devices: 27 us -> 0.02 us  [gather_y(): lax.all_gather(array, 'fsdp', axis=0, tiled=True, axis_index_groups=groups)]
    ppermute x17, waiting for transfers between devices: 30.2 us -> 55.4 us  [send_to(): return lax.ppermute(array, ('rep', 'fsdp'), pairs)]
    unnamed x19, local copies, waits for them, and re-layouts: 9.95 us -> 3.59 us
    ppermute x17, starting transfers between devices: 86.1 us -> 89.3 us  [send_to(): return lax.ppermute(array, ('rep', 'fsdp'), pairs)]
    pallas_call x1 -> x0, Pallas kernels: 2.36 us -> none  [fragment_term(): pl.pallas_call(kernel, in_specs=[pl.BlockSpec(memory_space=pltpu.VMEM)] *...]
  transfers between devices with their start and end apart: 19 -> 19, of which waited for: 8 -> 8; matrix products, arithmetic and copies ran while one was open for 13% -> 11% of each run, Pallas kernels for 4% -> 3%
where the time goes in v4:
time: 195 us; the launch traced here: 194 us
  starting transfers between devices  89.4 us (46%)
  waiting for transfers between devices  56.1 us (29%)
  between operations  14.6 us (7%)
  local copies, waits for them, and re-layouts  14 us (7%)
  Pallas kernels  11.3 us (6%)
  other arithmetic  8.22 us (4%)
    ppermute x17, starting transfers between devices, send_to(): return lax.ppermute(array, ('rep', 'fsdp'), pairs)  89.3 us
    ppermute x17, waiting for transfers between devices, send_to(): return lax.ppermute(array, ('rep', 'fsdp'), pairs)  55.4 us
    pallas_call x2, Pallas kernels, product(): pl.pallas_call(kernel, grid_spec=pltpu.PrefetchScalarGridSpec(num_scalar_...  11.3 us
  transfers between devices with their start and end apart: 19, of which 8 were waited for; matrix products, arithmetic and copies ran while one was open for 11% of the time, Pallas kernels for 3%

profile of v4, /device:TPU:1, one launch (start us, length us, event | category | flops | bytes accessed | tf_op | source)
XLA Modules:
  0.0 193.7 jit_solution(3506841476149388650)
XLA Ops:
  9.6 1.4 fusion.5
  11.7 12.4 %collective-permute-start.1 = (bf16[24,5120]{1,0:T(8,128)(2,1)}, bf16[24,5120]{1,0:T(8,128)(2,1)S(1)}, u32[]{:S(2)}, u32[]{:S(2)}) collective-permute-start(bf16[24,5120]{1,0:T(8,128)(2,1)} %broadcast_select_fusion.2), channel_id=1, source_target_pairs={{0,16},{16,0},{32,48},{48,32},{64,80},{80,64},{96,112},{112,96},{1... | collective-permute-start | bytes 737288 | tf_op jit(solution)/shard_map/ppermute | solution.py:37
  24.1 5.8 %collective-permute-start = (bf16[160,2560]{1,0:T(8,128)(2,1)}, bf16[160,2560]{1,0:T(8,128)(2,1)}, u32[]{:S(2)}, u32[]{:S(2)}) collective-permute-start(bf16[160,2560]{1,0:T(8,128)(2,1)} %bitcast.1), channel_id=1, source_target_pairs={{0,1},{16,17},{32,33},{48,49},{64,65},{80,81},{96,97},{112,113},{1... | collective-permute-start | bytes 2457608 | tf_op jit(solution)/shard_map/ppermute | solution.py:37
  31.5 4.6 %collective-permute-start.2 = (f32[24,2560]{1,0:T(8,128)}, f32[24,2560]{1,0:T(8,128)}, u32[]{:S(2)}, u32[]{:S(2)}) collective-permute-start(f32[24,2560]{1,0:T(8,128)} %slice_select_fusion.1), channel_id=1, source_target_pairs={{0,384},{16,400},{32,416},{48,432},{64,448},{80,464},{96,480},{112... | collective-permute-start | bytes 737288 | tf_op jit(solution)/shard_map/ppermute | solution.py:37
  39.5 2.9 %collective-permute-done.2 = f32[24,2560]{1,0:T(8,128)} collective-permute-done((f32[24,2560]{1,0:T(8,128)}, f32[24,2560]{1,0:T(8,128)}, u32[]{:S(2)}, u32[]{:S(2)}) %collective-permute-start.2) | collective-permute-done | bytes 245792 | tf_op jit(solution)/shard_map/ppermute | solution.py:37
  43.4 31.5 %collective-permute-done = bf16[160,2560]{1,0:T(8,128)(2,1)} collective-permute-done((bf16[160,2560]{1,0:T(8,128)(2,1)}, bf16[160,2560]{1,0:T(8,128)(2,1)}, u32[]{:S(2)}, u32[]{:S(2)}) %collective-permute-start) | collective-permute-done | bytes 819232 | tf_op jit(solution)/shard_map/ppermute | solution.py:37
  74.9 1.9 collective-permute-start.3
  76.9 1.8 fusion.8
  78.6 1.9 collective-permute-start.5
  80.6 3.4 %collective-permute-start.8 = (bf16[48,2560]{1,0:T(8,128)(2,1)}, bf16[48,2560]{1,0:T(8,128)(2,1)S(1)}, u32[]{:S(2)}, u32[]{:S(2)}) collective-permute-start(bf16[48,2560]{1,0:T(8,128)(2,1)} %get-tuple-element.29), channel_id=1, source_target_pairs={{0,2},{16,18},{32,34},{48,50},{64,66},{80,82},{96,98},{112,114},{1... | collective-permute-start | bytes 737288 | tf_op jit(solution)/shard_map/ppermute | solution.py:37
  83.9 1.9 slice.44
  85.9 15.4 %collective-permute-start.4 = (f32[24,1280]{1,0:T(8,128)S(1)}, f32[24,1280]{1,0:T(8,128)}, u32[]{:S(2)}, u32[]{:S(2)}) collective-permute-start(f32[24,1280]{1,0:T(8,128)S(1)} %select_add_fusion.2), channel_id=1, source_target_pairs={{0,32},{16,48},{32,0},{48,16},{64,96},{80,112},{96,64},{112,80},{1... | collective-permute-start | bytes 368648 | tf_op jit(solution)/shard_map/ppermute | solution.py:37
  101.3 1.4 copy.17.refs_0_
  102.8 1.3 copy.18.refs_0_
  105.8 4.6 %collective-permute-start.6 = (bf16[48,2560]{1,0:T(8,128)(2,1)}, bf16[48,2560]{1,0:T(8,128)(2,1)S(1)}, u32[]{:S(2)}, u32[]{:S(2)}) collective-permute-start(bf16[48,2560]{1,0:T(8,128)(2,1)} %collective-permute-done.5), channel_id=1, source_target_pairs={{0,14},{16,30},{32,46},{48,62},{64,78},{80,94},{96,110},{112,126},... | collective-permute-start | bytes 737288 | tf_op jit(solution)/shard_map/ppermute | solution.py:37
  110.4 1.9 collective-permute-start.9
  114.1 5.2 %collective-permute-start.7 = (bf16[48,2560]{1,0:T(8,128)(2,1)S(1)}, bf16[48,2560]{1,0:T(8,128)(2,1)}, u32[]{:S(2)}, u32[]{:S(2)}) collective-permute-start(bf16[48,2560]{1,0:T(8,128)(2,1)S(1)} %collective-permute-done.6), channel_id=1, source_target_pairs={{0,14},{16,30},{32,46},{48,62},{64,78},{80,94},{96,110},{112,126},... | collective-permute-start | bytes 737288 | tf_op jit(solution)/shard_map/ppermute | solution.py:37
  119.3 1.9 collective-permute-start.10
  121.3 8.6 %collective-permute-done.10 = bf16[48,2560]{1,0:T(8,128)(2,1)S(1)} collective-permute-done((bf16[48,2560]{1,0:T(8,128)(2,1)S(1)}, bf16[48,2560]{1,0:T(8,128)(2,1)S(1)}, u32[]{:S(2)}, u32[]{:S(2)}) %collective-permute-start.10) | collective-permute-done | bytes 245792 | tf_op jit(solution)/shard_map/ppermute | solution.py:37
  129.9 1.9 collective-permute-start.11
  131.8 5.3 %shard_map.85.refs_4_ = f32[256,2560]{1,0:T(8,128)} custom-call(s32[1]{0:T(128)} %bitcast.12.slot_ref, bf16[2,256,1280]{2,1,0:T(8,128)(2,1)} %copy.17.refs_0_, bf16[1280,2560]{1,0:T(8,128)(2,1)} %bitcast.30), custom_call_target="tpu_custom_call" | custom-call | flops 1677721600 | bytes 10485760 | tf_op jit(solution)/shard_map/pallas_call | solution.py:65
  137.2 1.9 collective-permute-start.12
  139.1 7.3 %collective-permute-start.13 = (f32[24,1280]{1,0:T(8,128)S(1)}, f32[24,1280]{1,0:T(8,128)S(1)}, u32[]{:S(2)}, u32[]{:S(2)}) collective-permute-start(f32[24,1280]{1,0:T(8,128)S(1)} %add.52), channel_id=1, source_target_pairs={{0,128},{16,144},{32,160},{48,176},{64,0},{80,16},{96,32},{112,48}... | collective-permute-start | bytes 368648 | tf_op jit(solution)/shard_map/ppermute | solution.py:37
  147.3 1.7 collective-permute-done.13
  149.1 1.9 collective-permute-start.14
  152.0 3.1 %collective-permute-done.14 = f32[24,1280]{1,0:T(8,128)S(1)} collective-permute-done((f32[24,1280]{1,0:T(8,128)S(1)}, f32[24,1280]{1,0:T(8,128)S(1)}, u32[]{:S(2)}, u32[]{:S(2)}) %collective-permute-start.14) | collective-permute-done | bytes 122912 | tf_op jit(solution)/shard_map/ppermute | solution.py:37
  155.2 3.1 %collective-permute-start.15 = (f32[24,2560]{1,0:T(8,128)S(1)}, f32[24,2560]{1,0:T(8,128)S(1)}, u32[]{:S(2)}, u32[]{:S(2)}) collective-permute-start(f32[24,2560]{1,0:T(8,128)S(1)} %pad_maximum_fusion.1), channel_id=1, source_target_pairs={{0,384},{16,400},{32,416},{48,432},{64,448},{80,464},{96,480},{112... | collective-permute-start | bytes 737288 | tf_op jit(solution)/shard_map/ppermute | solution.py:37
  158.3 5.3 %collective-permute-done.15 = f32[24,2560]{1,0:T(8,128)S(1)} collective-permute-done((f32[24,2560]{1,0:T(8,128)S(1)}, f32[24,2560]{1,0:T(8,128)S(1)}, u32[]{:S(2)}, u32[]{:S(2)}) %collective-permute-start.15) | collective-permute-done | bytes 245792 | tf_op jit(solution)/shard_map/ppermute | solution.py:37
  163.8 14.1 %collective-permute-start.16 = (f32[24,5120]{1,0:T(8,128)S(1)}, f32[24,5120]{1,0:T(8,128)S(1)}, u32[]{:S(2)}, u32[]{:S(2)}) collective-permute-start(f32[24,5120]{1,0:T(8,128)S(1)} %pad_maximum_fusion), channel_id=1, source_target_pairs={{0,16},{16,0},{32,48},{48,32},{64,80},{80,64},{96,112},{112,96},{1... | collective-permute-start | bytes 1474568 | tf_op jit(solution)/shard_map/ppermute | solution.py:37
  178.0 1.4 collective-permute-done.16
  179.5 1.4 fusion.3
  180.9 6.0 %shard_map.86 = bf16[256,2560]{1,0:T(8,128)(2,1)} custom-call(s32[1]{0:T(128)} %bitcast.slot_ref, bf16[2,256,896]{2,1,0:T(8,128)(2,1)} %copy.18.refs_0_, bf16[896,2560]{1,0:T(8,128)(2,1)} %all-gather.4.cloned.1.call-done.refs_1_, bf16[1,256,384]{2,1,0:T(8,128)(2,1)} %copy.19.refs_2_, bf16[384,2560]{1,0:T(8,128)(2,1)} %copy-done.1, f32[256,2560]{1,0:T(8,128)} %shard_map.85.refs_4_), custom_call_target="tpu_custom_call" | custom-call | flops 1677721600 | bytes 10485760 | tf_op jit(solution)/shard_map/pallas_call | solution.py:65
  (62 shorter events, 14.6 us)
Async XLA Ops:
  7.2 2.4 %copy-start.2 = (bf16[48,5120]{1,0:T(8,128)(2,1)S(1)}, bf16[48,5120]{1,0:T(8,128)(2,1)}, u32[]{:S(2)}) copy-start(bf16[48,5120]{1,0:T(8,128)(2,1)} %param.8) | copy-start | bytes 1474564
  7.2 124.6 %all-gather.6.cloned.1.call-start = ((), (), s32[]{:S(2)}) async-start(), calls=%async_computation.1 | async-start | bytes 7372800 | tf_op jit(solution)/shard_map/all_gather | solution.py:110
  7.9 172.9 %all-gather.4.cloned.1.call-start = ((), (), s32[]{:S(2)}) async-start(), calls=%async_computation | async-start | bytes 5160960 | tf_op jit(solution)/shard_map/all_gather | solution.py:110
  9.5 20.5 %copy-start.4 = (bf16[256,2560]{1,0:T(8,128)(2,1)S(1)}, bf16[256,2560]{1,0:T(8,128)(2,1)}, u32[]{:S(2)}) copy-start(bf16[256,2560]{1,0:T(8,128)(2,1)} %param.6) | copy-start | bytes 3932164
  11.7 19.0 %collective-permute-start.1 = (bf16[24,5120]{1,0:T(8,128)(2,1)}, bf16[24,5120]{1,0:T(8,128)(2,1)S(1)}, u32[]{:S(2)}, u32[]{:S(2)}) collective-permute-start(bf16[24,5120]{1,0:T(8,128)(2,1)} %broadcast_select_fusion.2), channel_id=1, source_target_pairs={{0,16},{16,0},{32,48},{48,32},{64,80},{80,64},{96,112},{112,96},{1... | collective-permute-start | bytes 737288 | tf_op jit(solution)/shard_map/ppermute | solution.py:37
  24.1 50.8 %collective-permute-start = (bf16[160,2560]{1,0:T(8,128)(2,1)}, bf16[160,2560]{1,0:T(8,128)(2,1)}, u32[]{:S(2)}, u32[]{:S(2)}) collective-permute-start(bf16[160,2560]{1,0:T(8,128)(2,1)} %bitcast.1), channel_id=1, source_target_pairs={{0,1},{16,17},{32,33},{48,49},{64,65},{80,81},{96,97},{112,113},{1... | collective-permute-start | bytes 2457608 | tf_op jit(solution)/shard_map/ppermute | solution.py:37
  31.5 11.0 %collective-permute-start.2 = (f32[24,2560]{1,0:T(8,128)}, f32[24,2560]{1,0:T(8,128)}, u32[]{:S(2)}, u32[]{:S(2)}) collective-permute-start(f32[24,2560]{1,0:T(8,128)} %slice_select_fusion.1), channel_id=1, source_target_pairs={{0,384},{16,400},{32,416},{48,432},{64,448},{80,464},{96,480},{112... | collective-permute-start | bytes 737288 | tf_op jit(solution)/shard_map/ppermute | solution.py:37
  38.1 1.4 slice-start
  74.9 10.9 %collective-permute-start.3 = (f32[24,1280]{1,0:T(8,128)S(1)}, f32[24,1280]{1,0:T(8,128)S(1)}, u32[]{:S(2)}, u32[]{:S(2)}) collective-permute-start(f32[24,1280]{1,0:T(8,128)S(1)} %slice_select_fusion.2), channel_id=1, source_target_pairs={{0,192},{16,208},{32,224},{48,240},{64,256},{80,272},{96,288},{112... | collective-permute-start | bytes 368648 | tf_op jit(solution)/shard_map/ppermute | solution.py:37
  78.6 27.2 %collective-permute-start.5 = (bf16[48,2560]{1,0:T(8,128)(2,1)}, bf16[48,2560]{1,0:T(8,128)(2,1)}, u32[]{:S(2)}, u32[]{:S(2)}) collective-permute-start(bf16[48,2560]{1,0:T(8,128)(2,1)} %get-tuple-element.29), channel_id=1, source_target_pairs={{0,14},{16,30},{32,46},{48,62},{64,78},{80,94},{96,110},{112,126},... | collective-permute-start | bytes 737288 | tf_op jit(solution)/shard_map/ppermute | solution.py:37
  80.6 29.9 %collective-permute-start.8 = (bf16[48,2560]{1,0:T(8,128)(2,1)}, bf16[48,2560]{1,0:T(8,128)(2,1)S(1)}, u32[]{:S(2)}, u32[]{:S(2)}) collective-permute-start(bf16[48,2560]{1,0:T(8,128)(2,1)} %get-tuple-element.29), channel_id=1, source_target_pairs={{0,2},{16,18},{32,34},{48,50},{64,66},{80,82},{96,98},{112,114},{1... | collective-permute-start | bytes 737288 | tf_op jit(solution)/shard_map/ppermute | solution.py:37
  85.9 19.0 %collective-permute-start.4 = (f32[24,1280]{1,0:T(8,128)S(1)}, f32[24,1280]{1,0:T(8,128)}, u32[]{:S(2)}, u32[]{:S(2)}) collective-permute-start(f32[24,1280]{1,0:T(8,128)S(1)} %select_add_fusion.2), channel_id=1, source_target_pairs={{0,32},{16,48},{32,0},{48,16},{64,96},{80,112},{96,64},{112,80},{1... | collective-permute-start | bytes 368648 | tf_op jit(solution)/shard_map/ppermute | solution.py:37
  102.8 9.6 %copy-start = (bf16[384,2560]{1,0:T(8,128)(2,1)S(1)}, bf16[384,2560]{1,0:T(8,128)(2,1)}, u32[]{:S(2)}) copy-start(bf16[384,2560]{1,0:T(8,128)(2,1)} %get-tuple-element.30) | copy-start | bytes 5898244
  105.8 8.3 %collective-permute-start.6 = (bf16[48,2560]{1,0:T(8,128)(2,1)}, bf16[48,2560]{1,0:T(8,128)(2,1)S(1)}, u32[]{:S(2)}, u32[]{:S(2)}) collective-permute-start(bf16[48,2560]{1,0:T(8,128)(2,1)} %collective-permute-done.5), channel_id=1, source_target_pairs={{0,14},{16,30},{32,46},{48,62},{64,78},{80,94},{96,110},{112,126},... | collective-permute-start | bytes 737288 | tf_op jit(solution)/shard_map/ppermute | solution.py:37
  110.4 8.9 %collective-permute-start.9 = (bf16[48,2560]{1,0:T(8,128)(2,1)S(1)}, bf16[48,2560]{1,0:T(8,128)(2,1)S(1)}, u32[]{:S(2)}, u32[]{:S(2)}) collective-permute-start(bf16[48,2560]{1,0:T(8,128)(2,1)S(1)} %collective-permute-done.8), channel_id=1, source_target_pairs={{0,2},{16,18},{32,34},{48,50},{64,66},{80,82},{96,98},{112,114},{1... | collective-permute-start | bytes 737288 | tf_op jit(solution)/shard_map/ppermute | solution.py:37
  114.1 32.2 %collective-permute-start.7 = (bf16[48,2560]{1,0:T(8,128)(2,1)S(1)}, bf16[48,2560]{1,0:T(8,128)(2,1)}, u32[]{:S(2)}, u32[]{:S(2)}) collective-permute-start(bf16[48,2560]{1,0:T(8,128)(2,1)S(1)} %collective-permute-done.6), channel_id=1, source_target_pairs={{0,14},{16,30},{32,46},{48,62},{64,78},{80,94},{96,110},{112,126},... | collective-permute-start | bytes 737288 | tf_op jit(solution)/shard_map/ppermute | solution.py:37
  119.3 10.5 %collective-permute-start.10 = (bf16[48,2560]{1,0:T(8,128)(2,1)S(1)}, bf16[48,2560]{1,0:T(8,128)(2,1)S(1)}, u32[]{:S(2)}, u32[]{:S(2)}) collective-permute-start(bf16[48,2560]{1,0:T(8,128)(2,1)S(1)} %collective-permute-done.9), channel_id=1, source_target_pairs={{0,2},{16,18},{32,34},{48,50},{64,66},{80,82},{96,98},{112,114},{1... | collective-permute-start | bytes 737288 | tf_op jit(solution)/shard_map/ppermute | solution.py:37
  129.9 21.2 %collective-permute-start.11 = (bf16[48,2560]{1,0:T(8,128)(2,1)S(1)}, bf16[48,2560]{1,0:T(8,128)(2,1)}, u32[]{:S(2)}, u32[]{:S(2)}) collective-permute-start(bf16[48,2560]{1,0:T(8,128)(2,1)S(1)} %collective-permute-done.10), channel_id=1, source_target_pairs={{0,2},{16,18},{32,34},{48,50},{64,66},{80,82},{96,98},{112,114},{1... | collective-permute-start | bytes 737288 | tf_op jit(solution)/shard_map/ppermute | solution.py:37
  137.2 10.2 %collective-permute-start.12 = (f32[24,1280]{1,0:T(8,128)S(1)}, f32[24,1280]{1,0:T(8,128)S(1)}, u32[]{:S(2)}, u32[]{:S(2)}) collective-permute-start(f32[24,1280]{1,0:T(8,128)S(1)} %add.52), channel_id=1, source_target_pairs={{0,64},{16,80},{32,96},{48,112},{64,128},{80,144},{96,160},{112,17... | collective-permute-start | bytes 368648 | tf_op jit(solution)/shard_map/ppermute | solution.py:37
  139.1 10.0 %collective-permute-start.13 = (f32[24,1280]{1,0:T(8,128)S(1)}, f32[24,1280]{1,0:T(8,128)S(1)}, u32[]{:S(2)}, u32[]{:S(2)}) collective-permute-start(f32[24,1280]{1,0:T(8,128)S(1)} %add.52), channel_id=1, source_target_pairs={{0,128},{16,144},{32,160},{48,176},{64,0},{80,16},{96,32},{112,48}... | collective-permute-start | bytes 368648 | tf_op jit(solution)/shard_map/ppermute | solution.py:37
  149.1 6.0 %collective-permute-start.14 = (f32[24,1280]{1,0:T(8,128)S(1)}, f32[24,1280]{1,0:T(8,128)S(1)}, u32[]{:S(2)}, u32[]{:S(2)}) collective-permute-start(f32[24,1280]{1,0:T(8,128)S(1)} %select_add_fusion.1), channel_id=1, source_target_pairs={{0,192},{16,208},{32,224},{48,240},{64,256},{80,272},{96,288},{112... | collective-permute-start | bytes 368648 | tf_op jit(solution)/shard_map/ppermute | solution.py:37
  155.2 8.5 %collective-permute-start.15 = (f32[24,2560]{1,0:T(8,128)S(1)}, f32[24,2560]{1,0:T(8,128)S(1)}, u32[]{:S(2)}, u32[]{:S(2)}) collective-permute-start(f32[24,2560]{1,0:T(8,128)S(1)} %pad_maximum_fusion.1), channel_id=1, source_target_pairs={{0,384},{16,400},{32,416},{48,432},{64,448},{80,464},{96,480},{112... | collective-permute-start | bytes 737288 | tf_op jit(solution)/shard_map/ppermute | solution.py:37
  163.7 15.7 %copy-start.3 = (bf16[48,5120]{1,0:T(8,128)(2,1)S(1)}, bf16[48,5120]{1,0:T(8,128)(2,1)}, u32[]{:S(2)}) copy-start(bf16[48,5120]{1,0:T(8,128)(2,1)} %param.8) | copy-start | bytes 1474564
  163.7 15.7 %copy-start.5 = (f32[48,5120]{1,0:T(8,128)S(1)}, f32[48,5120]{1,0:T(8,128)}, u32[]{:S(2)}) copy-start(f32[48,5120]{1,0:T(8,128)} %param.11) | copy-start | bytes 2949124
  163.8 15.6 %collective-permute-start.16 = (f32[24,5120]{1,0:T(8,128)S(1)}, f32[24,5120]{1,0:T(8,128)S(1)}, u32[]{:S(2)}, u32[]{:S(2)}) collective-permute-start(f32[24,5120]{1,0:T(8,128)S(1)} %pad_maximum_fusion), channel_id=1, source_target_pairs={{0,16},{16,0},{32,48},{48,32},{64,80},{80,64},{96,112},{112,96},{1... | collective-permute-start | bytes 1474568 | tf_op jit(solution)/shard_map/ppermute | solution.py:37
  178.0 2.9 %copy-start.1 = (bf16[384,2560]{1,0:T(8,128)(2,1)}, bf16[384,2560]{1,0:T(8,128)(2,1)S(1)}, u32[]{:S(2)}) copy-start(bf16[384,2560]{1,0:T(8,128)(2,1)S(1)} %constant_dynamic-update-slice_fusion.refs_3_) | copy-start | bytes 5898244
Sparse Core Ops, SparseCore 0:
  10.4 95.6 all-gather.5
  108.4 70.7 all-gather.3
